TPU v7x, 32 devices: a whole 2x2x4 slice. The times are simulated.
32 devices in a mesh: dp: 4 (over y, x), ctx: 4 (over z), mp: 2 (over core).
Axes of the slice: x: 2, y: 2, z: 4, core: 2. Of those that a mesh axis runs over, the one named last changes fastest.
Arguments:
- tokens: bfloat16 [4096, 2304], P(('dp', 'ctx')), may hold values from -6 to 6
- cotangent: bfloat16 [4096, 2304], P(('dp', 'ctx')), may hold values from -6 to 6
- segments: int32 [4096], replicated, may hold values from 0 to 7, never falling along the last dimension, each value on 1 to 2048 neighbouring positions
- padding: int32 [4096], replicated, may hold values 0 or 1
- owners: int32 [7, 4], replicated, may hold values from 0 to 3, each once within a row
- gains: float32 [4, 2304], replicated, may hold values from 0.5 to 1.5
- gain_stats: float32 [4, 2304], replicated, may hold values from 4096 to 16384
- attention_input_master: float32 [2304, 4096], P('dp', ('ctx', 'mp')), may hold values from -0.125 to 0.125
- attn_out: float32 [2304, 2048], P('dp', ('ctx', 'mp')), may hold values from -0.5 to 0.5
- mlp_in: float32 [2304, 18432], P('dp', ('ctx', 'mp')), may hold values from -0.125 to 0.125
- mlp_out: float32 [2304, 9216], P('dp', ('ctx', 'mp')), may hold values from -0.0625 to 0.0625
- left_stats: float32 [4, 4, 2, 33, 576, 576], P('dp', 'ctx', 'mp'), may hold values from -104858 to 524288
- right_stats: float32 [4, 4, 2, 33, 128, 128], P('dp', 'ctx', 'mp'), may hold values from -471860 to 2359296
- left_roots: float32 [4, 4, 2, 33, 576, 576], P('dp', 'ctx', 'mp'), may hold values from -0.042044821 to 0.07357844
- right_roots: float32 [4, 4, 2, 33, 128, 128], P('dp', 'ctx', 'mp'), may hold values from -0.028867513 to 0.050518149
Outputs:
- block_out: bfloat16 [4096, 2304], P(('dp', 'ctx'))
- input_grad: float32 [4096, 2304], P(('dp', 'ctx'))
- grad_attn_in: float32 [2304, 4096], P('dp', ('ctx', 'mp'))
- grad_attn_out: float32 [2304, 2048], P('dp', ('ctx', 'mp'))
- grad_mlp_in: float32 [2304, 18432], P('dp', ('ctx', 'mp'))
- grad_mlp_out: float32 [2304, 9216], P('dp', ('ctx', 'mp'))
- new_attn_in: float32 [2304, 4096], P('dp', ('ctx', 'mp'))
- new_attn_out: float32 [2304, 2048], P('dp', ('ctx', 'mp'))
- new_mlp_in: float32 [2304, 18432], P('dp', ('ctx', 'mp'))
- new_mlp_out: float32 [2304, 9216], P('dp', ('ctx', 'mp'))
- new_left: float32 [4, 4, 2, 33, 576, 576], P('dp', 'ctx', 'mp')
- new_right: float32 [4, 4, 2, 33, 128, 128], P('dp', 'ctx', 'mp')
- gain_grad: float32 [4, 2304], replicated
- new_gain_stats: float32 [4, 2304], replicated
- new_gains: float32 [4, 2304], replicated
Inputs may be any that keep to these rules, and one draw needn't show every extreme that they name: `segments`: never falling along the tokens; a segment holds 1 to 2048 tokens, one exactly that many. `owners`: each row is a permutation.
All inputs are finite; a program needn't handle non-finite values.
Results may differ from a plain program's by a relative error of at most 0.02.
Values may be sent and summed in bfloat16 or wider, within the bound.
No kernel may reach another device: no remote copies, remote signals or barrier semaphores. Data moves between devices by JAX's collectives and lax.ppermute only.
A program may use at most 896 MiB of HBM per device.

v0:
```python
import math

import jax
import jax.numpy as jnp
from jax import lax
from jax.sharding import PartitionSpec as P

HEAD_SIZE = 256
QUERY_HEADS = 8
KEY_VALUE_HEADS = 4
PACKED_TOKENS = 4096
WINDOW = 1024
SUBW = 128


norm_eps = 1e-06
soft_cap = 50.0
stat_decay = 0.5
master_rate = 0.25
gain_rate = 0.3
rope_base = 10000.0
highest = lax.Precision.HIGHEST


def shifted(block, axis, distance):
    devices = range(lax.axis_size(axis))
    route = [(i - distance, i) for i in devices if i - distance in devices]
    return lax.ppermute(block, axis, route)


def normalize(values, gain):
    scale = lax.rsqrt(jnp.mean(values * values, axis=-1, keepdims=True) + norm_eps)
    normed = values * scale
    return (normed * gain, normed, scale)


def norm_back(normed, scale, gain, upstream):
    gain_part = jnp.sum(upstream * normed, axis=0)
    inner = upstream * gain
    return (scale * (inner - normed * jnp.mean(inner * normed, axis=-1, keepdims=True)), gain_part)


def rotation(positions):
    half = HEAD_SIZE // 2
    freqs = jnp.exp(jnp.arange(half, dtype=jnp.float32) * (-2.0 * math.log(rope_base) / HEAD_SIZE))
    angles = positions.astype(jnp.float32)[:, None] * freqs[None, :]
    return (jnp.cos(angles), jnp.sin(angles))


def rotate(values, cosine, sine):
    half = values.shape[-1] // 2
    first = values[..., :half]
    second = values[..., half:]
    cosine = cosine[:, None, :]
    sine = sine[:, None, :]
    return jnp.concatenate(
        [first * cosine - second * sine, second * cosine + first * sine], axis=-1
    )


def rotate_back(grads, cosine, sine):
    half = grads.shape[-1] // 2
    first = grads[..., :half]
    second = grads[..., half:]
    cosine = cosine[:, None, :]
    sine = sine[:, None, :]
    return jnp.concatenate(
        [first * cosine + second * sine, second * cosine - first * sine], axis=-1
    )


def inverse(order, count):
    slots = jnp.arange(count, dtype=jnp.int32)
    matches = order[None, :] == slots[:, None]
    return jnp.sum(jnp.where(matches, slots[None, :], 0), axis=1)


def from_width(left, whole, nctx, dblock):
    rows = left.shape[0]
    depth = whole.shape[0] // nctx
    blocks = whole.reshape(depth, nctx, dblock, whole.shape[2])
    columns = left.reshape(rows, depth, dblock)
    return jnp.einsum("tdr,dcrw->tcw", columns, blocks, preferred_element_type=jnp.float32)


def to_width(right, whole, nctx, dblock):
    rows = right.shape[0]
    depth = whole.shape[0] // nctx
    blocks = whole.reshape(depth, nctx, dblock, whole.shape[2])
    product = jnp.einsum("tcw,dcrw->tdr", right, blocks, preferred_element_type=jnp.float32)
    return product.reshape(rows, depth * dblock)


def model_sum(partial_sum):
    return lax.psum(partial_sum.astype(jnp.bfloat16), "mp").astype(jnp.float32)


def pair_term(left, right, nctx, dblock, count):
    rows = left.shape[0]
    cols = right.shape[2]
    depth = count // (nctx * dblock)
    columns = left
    columns = columns.reshape(rows, depth, dblock)
    return jnp.einsum("tdr,tcw->dcrw", columns, right, preferred_element_type=jnp.float32).reshape(
        count, cols
    )


def pair_terms(pairs, nctx, dblock, count):
    return jnp.concatenate(
        [pair_term(left, right, nctx, dblock, count) for left, right in pairs], axis=1
    )


def visibility(query_pos, key_pos, query_seg, key_seg, key_present):
    visible = (key_pos[None, :] <= query_pos[:, None]) & (
        query_pos[:, None] - key_pos[None, :] < WINDOW
    )
    visible = visible & (
        (query_pos // PACKED_TOKENS)[:, None] == (key_pos // PACKED_TOKENS)[None, :]
    )
    visible = visible & (query_seg[:, None] == key_seg[None, :])
    return visible & ((key_present[None, :] == 1) | (key_pos[None, :] == query_pos[:, None]))


def block_probs(query_part, key_part, visible):
    raw = jnp.einsum(
        "qd,kd->qk", query_part, key_part, preferred_element_type=jnp.float32
    ) * HEAD_SIZE ** (-0.5)
    bent = jnp.tanh(raw / soft_cap)
    capped = jnp.where(visible, soft_cap * bent, -1e30)
    top = jnp.max(capped, axis=-1, keepdims=True)
    expo = jnp.exp(capped - top)
    return (expo / jnp.sum(expo, axis=-1, keepdims=True), bent)


def body(
    tokens,
    cotangent,
    segments,
    padding,
    owners,
    gains,
    gain_stats,
    attention_input_master,
    attn_out,
    mlp_in,
    mlp_out,
    left_stats,
    right_stats,
    left_roots,
    right_roots,
):
    nctx = lax.axis_size("ctx")
    ctx_index = lax.axis_index("ctx")
    dp_index = lax.axis_index("dp")
    rows, width = tokens.shape
    group_rows = rows * nctx
    dblock = attention_input_master.shape[0]
    key_columns = (attention_input_master.shape[1] - HEAD_SIZE) // 2
    ffn_cols = mlp_out.shape[1]
    local_heads = nctx * key_columns // HEAD_SIZE
    head_group = QUERY_HEADS // KEY_VALUE_HEADS
    query_order = owners[0]
    key_order = owners[1]
    value_order = owners[2]
    out_order = owners[3]
    gate_order = owners[4]
    up_order = owners[5]
    down_order = owners[6]
    query_back = inverse(query_order, nctx)
    key_back = inverse(key_order, nctx)
    value_back = inverse(value_order, nctx)
    out_back = inverse(out_order, nctx)
    gate_back = inverse(gate_order, nctx)
    up_back = inverse(up_order, nctx)
    down_back = inverse(down_order, nctx)
    token_first = (dp_index * nctx + ctx_index) * rows
    token_pos = token_first + jnp.arange(rows, dtype=jnp.int32)
    cosine, sine = rotation(token_pos % PACKED_TOKENS)
    inputs = tokens.astype(jnp.float32)
    attn_in_low = attention_input_master.astype(jnp.bfloat16)[None]
    attn_out_low = attn_out.astype(jnp.bfloat16)[None]
    mlp_in_low = mlp_in.astype(jnp.bfloat16)[None]
    mlp_out_low = mlp_out.astype(jnp.bfloat16)[None]
    whole_in, whole_out, whole_up, whole_down = (
        lax.all_gather(attn_in_low, ("dp", "ctx"), axis=0, tiled=True),
        lax.all_gather(attn_out_low, ("dp", "ctx"), axis=0, tiled=True),
        lax.all_gather(mlp_in_low, ("dp", "ctx"), axis=0, tiled=True),
        lax.all_gather(mlp_out_low, ("dp", "ctx"), axis=0, tiled=True),
    )
    first_out, first_normed, first_scale = normalize(inputs, gains[0])
    hidden_in = first_out.astype(jnp.bfloat16)
    projected = from_width(hidden_in, whole_in, nctx, dblock)
    query_pre = projected[:, :, :HEAD_SIZE]
    key_before_rotation = projected[:, :, HEAD_SIZE : HEAD_SIZE + key_columns]
    value_projected = projected[:, :, HEAD_SIZE + key_columns :]
    query_low = rotate(query_pre, cosine, sine).astype(jnp.bfloat16)
    key_canon = jnp.take(key_before_rotation, key_back, axis=1).reshape(
        rows, local_heads, HEAD_SIZE
    )
    key_low = rotate(key_canon, cosine, sine).astype(jnp.bfloat16)
    value_low = (
        jnp.take(value_projected, value_back, axis=1)
        .reshape(rows, local_heads, HEAD_SIZE)
        .astype(jnp.bfloat16)
    )
    picked_head = query_order // head_group
    key_send = jnp.take(key_low, picked_head, axis=1)
    value_send = jnp.take(value_low, picked_head, axis=1)
    queries_h, keys_h, values_h = (
        lax.all_to_all(query_low, "ctx", split_axis=1, concat_axis=0, tiled=True),
        lax.all_to_all(key_send, "ctx", split_axis=1, concat_axis=0, tiled=True),
        lax.all_to_all(value_send, "ctx", split_axis=1, concat_axis=0, tiled=True),
    )
    queries_h = queries_h.reshape(group_rows, HEAD_SIZE)
    keys_h = keys_h.reshape(group_rows, HEAD_SIZE)
    values_h = values_h.reshape(group_rows, HEAD_SIZE)
    prev_keys, prev_values = shifted((keys_h, values_h), "dp", 1)
    keys_all = jnp.concatenate([prev_keys, keys_h], axis=0)
    values_all = jnp.concatenate([prev_values, values_h], axis=0)
    group_first = dp_index * group_rows
    query_pos_all = group_first + jnp.arange(group_rows, dtype=jnp.int32)
    key_pos_all = group_first - group_rows + jnp.arange(2 * group_rows, dtype=jnp.int32)
    segment_ext = jnp.concatenate([jnp.full((group_rows,), -1, jnp.int32), segments])
    present_ext = jnp.concatenate([jnp.zeros((group_rows,), jnp.int32), padding])
    key_seg_all = lax.dynamic_slice_in_dim(segment_ext, group_first, 2 * group_rows, 0)
    key_present_all = lax.dynamic_slice_in_dim(present_ext, group_first, 2 * group_rows, 0)
    query_seg_all = key_seg_all[group_rows:]
    block_rows = min(512, group_rows)
    blocks = group_rows // block_rows
    span = block_rows + WINDOW

    def block_inputs(number):
        first = number * block_rows
        key_first = group_rows + first - WINDOW
        query_part = lax.dynamic_slice_in_dim(queries_h, first, block_rows, 0)
        key_part = lax.dynamic_slice_in_dim(keys_all, key_first, span, 0)
        value_part = lax.dynamic_slice_in_dim(values_all, key_first, span, 0)
        visible = visibility(
            lax.dynamic_slice_in_dim(query_pos_all, first, block_rows, 0),
            lax.dynamic_slice_in_dim(key_pos_all, key_first, span, 0),
            lax.dynamic_slice_in_dim(query_seg_all, first, block_rows, 0),
            lax.dynamic_slice_in_dim(key_seg_all, key_first, span, 0),
            lax.dynamic_slice_in_dim(key_present_all, key_first, span, 0),
        )
        return (first, key_first, query_part, key_part, value_part, visible)

    def forward_block(number):
        first, key_first, query_part, key_part, value_part, visible = block_inputs(number)
        probs, bent = block_probs(query_part, key_part, visible)
        return jnp.einsum(
            "qk,kd->qd", probs.astype(jnp.bfloat16), value_part, preferred_element_type=jnp.float32
        )

    attended = lax.map(forward_block, jnp.arange(blocks, dtype=jnp.int32)).reshape(
        group_rows, HEAD_SIZE
    )
    attended_low = attended.astype(jnp.bfloat16)
    back_out = lax.all_to_all(
        attended_low[:, None, :], "ctx", split_axis=0, concat_axis=1, tiled=True
    )
    out_slots = jnp.take(back_out, query_back[out_order], axis=1)
    attn_part = to_width(out_slots, whole_out, nctx, dblock)
    attn = model_sum(attn_part)
    second_out, second_normed, second_scale = normalize(attn, gains[1])
    mixed = inputs + second_out
    third_out, third_normed, third_scale = normalize(mixed, gains[2])
    hidden_two = third_out.astype(jnp.bfloat16)
    gate_up = from_width(hidden_two, whole_up, nctx, dblock)
    gate = gate_up[:, :, :ffn_cols]
    upper = jnp.take(gate_up[:, :, ffn_cols:], up_back[gate_order], axis=1)
    gelu_value, gelu_pull = jax.vjp(lambda values: jax.nn.gelu(values, approximate=True), gate)
    active = (gelu_value * upper).astype(jnp.bfloat16)
    active_down = jnp.take(active, gate_back[down_order], axis=1)
    moved_part = to_width(active_down, whole_down, nctx, dblock)
    moved = model_sum(moved_part)
    fourth_out, fourth_normed, fourth_scale = normalize(moved, gains[3])
    block_out = (mixed + fourth_out).astype(jnp.bfloat16)
    upstream = cotangent.astype(jnp.float32)
    moved_grad, fourth_gain = norm_back(fourth_normed, fourth_scale, gains[3], upstream)
    moved_low = moved_grad.astype(jnp.bfloat16)
    active_grad = from_width(moved_low, whole_down, nctx, dblock)
    active_grad = jnp.take(active_grad, down_back[gate_order], axis=1)
    gate_grad = gelu_pull(active_grad * upper)[0].astype(jnp.bfloat16)
    upper_grad = (active_grad * gelu_value).astype(jnp.bfloat16)
    upper_slots = jnp.take(upper_grad, gate_back[up_order], axis=1)
    right_mlp = jnp.concatenate([gate_grad, upper_slots], axis=2)
    hidden_two_part = to_width(right_mlp, whole_up, nctx, dblock)
    hidden_two_grad = model_sum(hidden_two_part)
    mlp_summed = lax.psum_scatter(
        pair_terms(
            ((hidden_two, right_mlp), (moved_low, active_down)),
            nctx,
            dblock,
            dblock * lax.axis_size(("dp", "ctx")),
        ),
        ("dp", "ctx"),
        scatter_dimension=0,
        tiled=True,
    )
    mixed_part, third_gain = norm_back(third_normed, third_scale, gains[2], hidden_two_grad)
    mixed_grad = upstream + mixed_part
    attn_grad, second_gain = norm_back(second_normed, second_scale, gains[1], mixed_grad)
    attn_low = attn_grad.astype(jnp.bfloat16)
    out_grad = from_width(attn_low, whole_out, nctx, dblock)
    out_grad = jnp.take(out_grad, out_back[query_order], axis=1).astype(jnp.bfloat16)
    head_grad = lax.all_to_all(out_grad, "ctx", split_axis=1, concat_axis=0, tiled=True).reshape(
        group_rows, HEAD_SIZE
    )

    def backward_block(carried, number):
        key_acc, value_acc = carried
        first, key_first, query_part, key_part, value_part, visible = block_inputs(number)
        probs, bent = block_probs(query_part, key_part, visible)
        grad_part = lax.dynamic_slice_in_dim(head_grad, first, block_rows, 0)
        prob_grad = jnp.einsum(
            "qd,kd->qk", grad_part, value_part, preferred_element_type=jnp.float32
        )
        delta = jnp.sum(probs * prob_grad, axis=-1, keepdims=True)
        score_grad = (probs * (prob_grad - delta) * (1.0 - bent * bent)).astype(jnp.bfloat16)
        query_grad = jnp.einsum(
            "qk,kd->qd", score_grad, key_part, preferred_element_type=jnp.float32
        ) * HEAD_SIZE ** (-0.5)
        key_grad = jnp.einsum(
            "qk,qd->kd", score_grad, query_part, preferred_element_type=jnp.float32
        ) * HEAD_SIZE ** (-0.5)
        value_grad = jnp.einsum(
            "qk,qd->kd", probs.astype(jnp.bfloat16), grad_part, preferred_element_type=jnp.float32
        )
        key_acc = lax.dynamic_update_slice_in_dim(
            key_acc, lax.dynamic_slice_in_dim(key_acc, key_first, span, 0) + key_grad, key_first, 0
        )
        value_acc = lax.dynamic_update_slice_in_dim(
            value_acc,
            lax.dynamic_slice_in_dim(value_acc, key_first, span, 0) + value_grad,
            key_first,
            0,
        )
        return ((key_acc, value_acc), query_grad)

    empty = jnp.zeros((2 * group_rows, HEAD_SIZE), jnp.float32)
    (key_acc, value_acc), query_grads = lax.scan(
        backward_block, (empty, empty), jnp.arange(blocks, dtype=jnp.int32)
    )
    query_grads = query_grads.reshape(group_rows, HEAD_SIZE)
    recv_keys, recv_values = (
        shifted(key_acc[:group_rows].astype(jnp.bfloat16), "dp", -1).astype(jnp.float32),
        shifted(value_acc[:group_rows].astype(jnp.bfloat16), "dp", -1).astype(jnp.float32),
    )
    key_total = (key_acc[group_rows:] + recv_keys).astype(jnp.bfloat16)
    value_total = (value_acc[group_rows:] + recv_values).astype(jnp.bfloat16)
    query_total = query_grads.astype(jnp.bfloat16)
    query_tok, key_tok, value_tok = (
        lax.all_to_all(query_total[:, None, :], "ctx", split_axis=0, concat_axis=1, tiled=True),
        lax.all_to_all(key_total[:, None, :], "ctx", split_axis=0, concat_axis=1, tiled=True),
        lax.all_to_all(value_total[:, None, :], "ctx", split_axis=0, concat_axis=1, tiled=True),
    )
    query_slots = rotate_back(query_tok.astype(jnp.float32), cosine, sine).astype(jnp.bfloat16)
    mixing = (picked_head[:, None] == jnp.arange(local_heads, dtype=jnp.int32)[None, :]).astype(
        jnp.bfloat16
    )
    key_canon_grad = jnp.einsum("tch,cl->tlh", key_tok, mixing, preferred_element_type=jnp.float32)
    key_canon_grad = rotate_back(key_canon_grad, cosine, sine).reshape(rows, nctx, key_columns)
    key_slots = jnp.take(key_canon_grad, key_order, axis=1).astype(jnp.bfloat16)
    value_canon_grad = jnp.einsum(
        "tch,cl->tlh", value_tok, mixing, preferred_element_type=jnp.float32
    ).reshape(rows, nctx, key_columns)
    value_slots = jnp.take(value_canon_grad, value_order, axis=1).astype(jnp.bfloat16)
    right_attn = jnp.concatenate([query_slots, key_slots, value_slots], axis=2)
    hidden_part = to_width(right_attn, whole_in, nctx, dblock)
    hidden_grad = model_sum(hidden_part)
    input_part, first_gain = norm_back(first_normed, first_scale, gains[0], hidden_grad)
    input_grad = mixed_grad + input_part
    attn_summed = lax.psum_scatter(
        pair_terms(
            ((hidden_in, right_attn), (attn_low, out_slots)),
            nctx,
            dblock,
            dblock * lax.axis_size(("dp", "ctx")),
        ),
        ("dp", "ctx"),
        scatter_dimension=0,
        tiled=True,
    )
    summed = jnp.concatenate([attn_summed, mlp_summed], axis=1)
    gain_grad = lax.psum(
        jnp.stack([first_gain, second_gain, third_gain, fourth_gain], axis=0), ("dp", "ctx")
    )
    masters = (attention_input_master, attn_out, mlp_in, mlp_out)
    grads = []
    column = 0
    for master in masters:
        grads.append(summed[:, column : column + master.shape[1]])
        column = column + master.shape[1]
    pieces = [
        jnp.transpose(grad.reshape(dblock, grad.shape[1] // SUBW, SUBW), (1, 0, 2))
        for grad in grads
    ]
    stacked = jnp.concatenate(pieces, axis=0)
    left_now = left_stats.reshape(left_stats.shape[3:])
    right_now = right_stats.reshape(right_stats.shape[3:])
    new_left = stat_decay * left_now + (1.0 - stat_decay) * jnp.einsum(
        "brs,bqs->brq", stacked, stacked, precision=highest
    )
    new_right = stat_decay * right_now + (1.0 - stat_decay) * jnp.einsum(
        "brs,brq->bsq", stacked, stacked, precision=highest
    )
    step = jnp.einsum(
        "brq,bqs->brs", left_roots.reshape(left_roots.shape[3:]), stacked, precision=highest
    )
    step = jnp.einsum(
        "brs,bsq->brq", step, right_roots.reshape(right_roots.shape[3:]), precision=highest
    )
    updated = []
    offset = 0
    for master in masters:
        count = master.shape[1] // SUBW
        part = step[offset : offset + count]
        updated.append(
            master - master_rate * jnp.transpose(part, (1, 0, 2)).reshape(dblock, master.shape[1])
        )
        offset = offset + count
    new_gain_stats = stat_decay * gain_stats + (1.0 - stat_decay) * gain_grad * gain_grad
    new_gains = gains - gain_rate * gain_grad * lax.rsqrt(new_gain_stats)
    return (
        block_out,
        input_grad,
        grads[0],
        grads[1],
        grads[2],
        grads[3],
        updated[0],
        updated[1],
        updated[2],
        updated[3],
        new_left.reshape(left_stats.shape),
        new_right.reshape(right_stats.shape),
        gain_grad,
        new_gain_stats,
        new_gains,
    )


def solution(mesh):
    return jax.shard_map(
        body,
        mesh=mesh,
        in_specs=(
            P(("dp", "ctx"), None),
            P(("dp", "ctx"), None),
            P(),
            P(),
            P(),
            P(),
            P(),
            P("dp", ("ctx", "mp")),
            P("dp", ("ctx", "mp")),
            P("dp", ("ctx", "mp")),
            P("dp", ("ctx", "mp")),
            P("dp", "ctx", "mp", None, None, None),
            P("dp", "ctx", "mp", None, None, None),
            P("dp", "ctx", "mp", None, None, None),
            P("dp", "ctx", "mp", None, None, None),
        ),
        out_specs=(
            P(("dp", "ctx"), None),
            P(("dp", "ctx"), None),
            P("dp", ("ctx", "mp")),
            P("dp", ("ctx", "mp")),
            P("dp", ("ctx", "mp")),
            P("dp", ("ctx", "mp")),
            P("dp", ("ctx", "mp")),
            P("dp", ("ctx", "mp")),
            P("dp", ("ctx", "mp")),
            P("dp", ("ctx", "mp")),
            P("dp", "ctx", "mp", None, None, None),
            P("dp", "ctx", "mp", None, None, None),
            P(),
            P(),
            P(),
        ),
        check_vma=False,
    )
```

profile of v0, /device:TPU:0, one launch (start us, length us, event | category | flops | bytes accessed | tf_op | source)
XLA Modules:
  0.0 3786.6 jit_solution(11369651215358378900)
XLA Ops:
  18.6 118.0 %all-gather.9.cloned.1.call-done = bf16[9216,512]{1,0:T(8,128)(2,1)} async-done(((bf16[576,512]{1,0:T(8,128)(2,1)}), bf16[9216,512]{1,0:T(8,128)(2,1)}) %all-gather.9.cloned.1.call-update) | async-done | bytes 9437200 | tf_op jit(solution)/shard_map/all_gather | solution.py:187
  175.3 25.7 all_to_all.123
  209.3 20.8 all-to-all-done.2
  249.8 15.9 while.34
  311.4 11.8 all-reduce.7.cloned.1.call-done
  330.9 230.9 %all-gather.15.cloned.1.call-done = bf16[9216,1152]{1,0:T(8,128)(2,1)} async-done(((bf16[576,1152]{1,0:T(8,128)(2,1)}), bf16[9216,1152]{1,0:T(8,128)(2,1)}) %all-gather.15.cloned.1.call-update) | async-done | bytes 21233680 | tf_op jit(solution)/shard_map/all_gather | solution.py:190
  561.9 16.0 copy.174
  577.9 420.8 %all-gather.13.cloned.1.call-done = bf16[9216,2304]{1,0:T(8,128)(2,1)} async-done(((bf16[576,2304]{1,0:T(8,128)(2,1)}), bf16[9216,2304]{1,0:T(8,128)(2,1)}) %all-gather.13.cloned.1.call-update) | async-done | bytes 42467344 | tf_op jit(solution)/shard_map/all_gather | solution.py:189
  998.7 21.4 convolution_bitcast_fusion.3
  1039.8 12.0 fusion.68
  1052.8 28.7 copy.177
  1090.5 11.8 convolution_bitcast_fusion.4
  1107.7 8.5 fusion.62
  1123.6 19.1 fusion.66
  1143.5 17.7 all-reduce.11.cloned.1.call-done
  1188.6 15.0 all-to-all-done.4
  1207.5 31.6 while.35
  1270.0 8.3 copy.187
  1318.7 9.9 convolution_bitcast_fusion.2
  1336.4 9.7 pad_maximum_fusion.1
  1347.4 19.5 convolution_bitcast_fusion.1
  1366.9 31.2 copy.191
  1398.1 32.0 convolution_bitcast_fusion
  1430.0 58.0 %copy.190 = f32[4,4,576,2304]{3,2,1,0:T(8,128)} copy(f32[4,4,576,2304]{3,2,0,1:T(8,128)} %convolution_bitcast_fusion) | data formatting | bytes 169869312 | tf_op jit(solution)/shard_map/tdr,tcw->dcrw/transpose | solution.py:104
  1488.0 86.2 %pad_maximum_fusion = f32[9216,3456]{1,0:T(8,128)} fusion(f32[9216,1152]{1,0:T(8,128)} %bitcast.339, f32[9216,2304]{1,0:T(8,128)} %bitcast.103), kind=kLoop, calls=%fused_computation.103 | loop fusion | flops 31850496 | bytes 254803968 | tf_op jit(solution)/shard_map/concatenate | solution.py:110
  1586.7 82.3 %psum.39 = f32[4,2304]{1,0:T(4,128)S(1)} all-reduce(f32[4,2304]{1,0:T(4,128)S(1)} %pad_maximum_fusion.19), channel_id=1, replica_groups=mesh['dp'=4,'ctx'=4,'mp'=2] {'dp','ctx'}, use_global_device_ids=true, to_apply=%region_34.39 | all-reduce | flops 9216 | bytes 73728 | tf_op jit(solution)/shard_map/psum | solution.py:387
  1673.8 76.1 %reduce-scatter.3.cloned.1.call-done = f32[576,768]{1,0:T(8,128)} async-done(((f32[9216,768]{1,0:T(8,128)}), f32[576,768]{1,0:T(8,128)}) %reduce-scatter.3.cloned.1.call-update) | async-done | bytes 1769488 | tf_op jit(solution)/shard_map/reduce_scatter | solution.py:375
  1754.1 1813.2 %reduce-scatter.5.cloned.1.call-done = f32[576,3456]{1,0:T(8,128)} async-done(((f32[9216,3456]{1,0:T(8,128)}), f32[576,3456]{1,0:T(8,128)}) %reduce-scatter.5.cloned.1.call-update) | async-done | bytes 7962640 | tf_op jit(solution)/shard_map/reduce_scatter | solution.py:291
  3595.7 51.1 %fusion.53 = f32[33,128,576]{1,2,0:T(8,128)} fusion(f32[1,1,1,33,576,576]{5,4,3,2,1,0:T(8,128)} %param.40, f32[9,576,128]{2,1,0:T(8,128)} %bitcast.352, f32[18,576,128]{2,1,0:T(8,128)} %bitcast.343, f32[2,576,128]{2,1,0:T(8,128)} %bitcast_bitcast_fusion.1, f32[4,576,128]{2,1,0:T(8,128)S(1)} %bitcast_bitcast_fusion), kind=kOutput, calls=%fused_computation.107 | convolution fusion | flops 16824360960 | bytes 63258624 | tf_op jit(solution)/shard_map/brq,bqs->brs/dot_general | solution.py:409
  3646.7 13.1 fusion.112
  3698.4 55.1 %fusion.52 = f32[1,1,1,33,576,576]{5,4,3,2,1,0:T(8,128)} fusion(f32[1,1,1,33,576,576]{5,4,3,2,1,0:T(8,128)} %param.38, f32[9,576,128]{2,1,0:T(8,128)} %bitcast.353, f32[18,576,128]{2,1,0:T(8,128)} %bitcast.344, f32[2,576,128]{2,1,0:T(8,128)} %bitcast_bitcast_fusion.1, f32[4,576,128]{2,1,0:T(8,128)} %copy-done.14), kind=kOutput, calls=%fused_computation.106 | convolution fusion | flops 16846258176 | bytes 97320960 | tf_op jit(solution)/shard_map/brs,bqs->brq/dot_general | solution.py:403
  3753.5 26.1 fusion.111
  (453 shorter events, 418.0 us)
Async XLA Ops:
  7.2 3639.6 %copy-start = (f32[1,1,1,33,128,128]{5,4,3,2,1,0:T(8,128)S(1)}, f32[1,1,1,33,128,128]{5,4,3,2,1,0:T(8,128)}, u32[]{:S(2)}) copy-start(f32[1,1,1,33,128,128]{5,4,3,2,1,0:T(8,128)} %param.41) | copy-start | bytes 6488068
  7.2 129.3 %all-gather.9.cloned.1.call-start = ((), (), s32[]{:S(2)}) async-start(), calls=%async_computation.16 | async-start | bytes 10027008 | tf_op jit(solution)/shard_map/all_gather | solution.py:187
  9.6 267.4 %all-gather.11.cloned.1.call-start = ((), (), s32[]{:S(2)}) async-start(), calls=%async_computation.17 | async-start | bytes 5013504 | tf_op jit(solution)/shard_map/all_gather | solution.py:188
  18.6 147.6 %copy-start.24 = (f32[256,128]{1,0:T(8,128)}, f32[256,128]{1,0:T(8,128)S(1)}, u32[]{:S(2)}) copy-start(f32[256,128]{1,0:T(8,128)S(1)} %get-tuple-element.759) | copy-start | bytes 393220
  175.3 61.0 %copy-start.54 = (s32[4096]{0:T(1024)S(1)}, s32[4096]{0:T(1024)}, u32[]{:S(2)}) copy-start(s32[4096]{0:T(1024)} %param.29) | copy-start | bytes 49156
  175.3 61.0 %copy-start.61 = (s32[4096]{0:T(1024)S(1)}, s32[4096]{0:T(1024)}, u32[]{:S(2)}) copy-start(s32[4096]{0:T(1024)} %param.30) | copy-start | bytes 49156
  201.1 29.0 all-to-all-start.2
  205.2 31.2 collective-permute-start
  230.1 18.9 all-to-all-start
  234.3 12.4 collective-permute-start.1
  270.9 17.8 all-to-all-start.3
  275.6 47.5 %all-reduce.7.cloned.1.call-start = ((), (), s32[]{:S(2)}) async-start(), calls=%async_computation.10 | async-start | bytes 2359296 | tf_op jit(solution)/shard_map/psum | solution.py:95
  301.6 260.3 %all-gather.15.cloned.1.call-start = ((), (), s32[]{:S(2)}) async-start(), calls=%async_computation.19 | async-start | bytes 22560768 | tf_op jit(solution)/shard_map/all_gather | solution.py:190
  304.6 694.1 %all-gather.13.cloned.1.call-start = ((), (), s32[]{:S(2)}) async-start(), calls=%async_computation.18 | async-start | bytes 45121536 | tf_op jit(solution)/shard_map/all_gather | solution.py:189
  309.0 772.6 %all-reduce.9.cloned.1.call-start = ((), (), s32[]{:S(2)}) async-start(), calls=%async_computation.11 | async-start | bytes 2359296 | tf_op jit(solution)/shard_map/psum | solution.py:95
  311.4 728.5 %copy-start.62 = (pred[4]{0:T(512)(128)(4,1)}, pred[4]{0:T(512)(128)(4,1)S(1)}, u32[]{:S(2)}) copy-start(pred[4]{0:T(512)(128)(4,1)S(1)} %compare_and_fusion.4) | copy-start | bytes 16
  1051.9 109.3 %all-reduce.11.cloned.1.call-start = ((), (), s32[]{:S(2)}) async-start(), calls=%async_computation.12 | async-start | bytes 2359296 | tf_op jit(solution)/shard_map/psum | solution.py:95
  1183.7 19.9 all-to-all-start.4
  1241.1 15.2 collective-permute-start.3
  1247.0 18.3 all-to-all-start.5
  1253.3 25.0 collective-permute-start.2
  1265.3 19.8 all-to-all-start.7
  1285.1 19.3 all-to-all-start.6
  1290.2 294.3 %all-reduce.13.cloned.1.call-start = ((), (), s32[]{:S(2)}) async-start(), calls=%async_computation.13 | async-start | bytes 2359296 | tf_op jit(solution)/shard_map/psum | solution.py:95
  1318.6 431.2 %reduce-scatter.3.cloned.1.call-start = ((), (), s32[]{:S(2)}) async-start(), calls=%async_computation.14 | async-start | bytes 30081024 | tf_op jit(solution)/shard_map/reduce_scatter | solution.py:375
  1346.1 2221.2 %reduce-scatter.5.cloned.1.call-start = ((), (), s32[]{:S(2)}) async-start(), calls=%async_computation.15 | async-start | bytes 135364608 | tf_op jit(solution)/shard_map/reduce_scatter | solution.py:291
  1366.9 31.2 copy-start.16
  1366.9 31.2 copy-start.18
  1584.4 84.6 %copy-start.52 = (f32[4,2304]{1,0:T(4,128)S(1)}, f32[4,2304]{1,0:T(4,128)}, u32[]{:S(2)}) copy-start(f32[4,2304]{1,0:T(4,128)} %param.32) | copy-start | bytes 110596
  1584.4 84.6 %copy-start.58 = (f32[4,2304]{1,0:T(4,128)S(1)}, f32[4,2304]{1,0:T(4,128)}, u32[]{:S(2)}) copy-start(f32[4,2304]{1,0:T(4,128)} %param.33) | copy-start | bytes 110596
  1754.1 1841.5 %copy-start.14 = (f32[4,576,128]{2,1,0:T(8,128)}, f32[4,576,128]{2,1,0:T(8,128)S(1)}, u32[]{:S(2)}) copy-start(f32[4,576,128]{2,1,0:T(8,128)S(1)} %bitcast_bitcast_fusion) | copy-start | bytes 3538948
  3698.4 55.1 %copy-start.8 = (f32[576,9,128]{2,0,1:T(8,128)S(1)}, f32[576,9,128]{2,0,1:T(8,128)}, u32[]{:S(2)}) copy-start(f32[576,9,128]{2,0,1:T(8,128)} %copy.197) | copy-start | bytes 7962628
  (75 other events, 396.2 us)
Sparse Core Ops, SparseCore 0:
  11.4 125.1 all-gather.8
  139.9 91.8 all-gather.10
  301.7 21.3 all-reduce.6
  326.7 235.1 all-gather.14
  565.5 433.2 all-gather.12
  1052.0 17.9 all-reduce.8
  1142.9 18.2 all-reduce.10
  1318.7 22.8 all-reduce.12
  1347.4 402.3 reduce-scatter.2
  1755.7 1811.5 reduce-scatter.4
where the time goes:
time: 3800 us; the launch traced here: 3790 us
  waiting for transfers between devices  2740 us (72%)
  local copies, waits for them, and re-layouts  332 us (9%)
  matrix products  326 us (9%)
  other arithmetic  219 us (6%)
  blocking collectives  108 us (3%)
  starting transfers between devices  39.6 us (1%)
    reduce_scatter x1, waiting for transfers between devices, body(): lax.psum_scatter(pair_terms(((hidden_two, right_mlp), (moved_low, active_...  1810 us
    all_gather x1, waiting for transfers between devices, body(): lax.all_gather(mlp_in_low, ('dp', 'ctx'), axis=0, tiled=True)  421 us
    all_gather x1, waiting for transfers between devices, body(): lax.all_gather(mlp_out_low, ('dp', 'ctx'), axis=0, tiled=True)  231 us
    all_gather x1, waiting for transfers between devices, body(): lax.all_gather(attn_in_low, ('dp', 'ctx'), axis=0, tiled=True)  118 us
    transpose x4, local copies, waits for them, and re-layouts, pair_term(): jnp.einsum('tdr,tcw->dcrw', columns, right, preferred_element_type=jnp.fl...  102 us
    concatenate x2, other arithmetic, pair_terms(): jnp.concatenate([pair_term(left, right, nctx, dblock, count) for left, ri...  96 us
    psum x1, blocking collectives, body(): lax.psum(jnp.stack([first_gain, second_gain, third_gain, fourth_gain], ax...  82.3 us
    reduce_scatter x1, waiting for transfers between devices, body(): lax.psum_scatter(pair_terms(((hidden_in, right_attn), (attn_low, out_slot...  76.1 us
  transfers between devices with their start and end apart: 21, of which 13 were waited for; matrix products, arithmetic and copies ran while one was open for 12% of the time, Pallas kernels for 0%

commit v1 on v0

v1 whole, which is shorter than its diff:
```python
import math

import jax
import jax.numpy as jnp
from jax import lax
from jax.sharding import PartitionSpec as P

HEAD_SIZE = 256
QUERY_HEADS = 8
KEY_VALUE_HEADS = 4
PACKED_TOKENS = 4096
WINDOW = 1024
SUBW = 128


norm_eps = 1e-06
soft_cap = 50.0
stat_decay = 0.5
master_rate = 0.25
gain_rate = 0.3
rope_base = 10000.0
highest = lax.Precision.HIGHEST


def shifted(block, axis, distance):
    devices = range(lax.axis_size(axis))
    route = [(i - distance, i) for i in devices if i - distance in devices]
    return lax.ppermute(block, axis, route)


def normalize(values, gain):
    scale = lax.rsqrt(jnp.mean(values * values, axis=-1, keepdims=True) + norm_eps)
    normed = values * scale
    return (normed * gain, normed, scale)


def norm_back(normed, scale, gain, upstream):
    gain_part = jnp.sum(upstream * normed, axis=0)
    inner = upstream * gain
    return (scale * (inner - normed * jnp.mean(inner * normed, axis=-1, keepdims=True)), gain_part)


def rotation(positions):
    half = HEAD_SIZE // 2
    freqs = jnp.exp(jnp.arange(half, dtype=jnp.float32) * (-2.0 * math.log(rope_base) / HEAD_SIZE))
    angles = positions.astype(jnp.float32)[:, None] * freqs[None, :]
    return (jnp.cos(angles), jnp.sin(angles))


def rotate(values, cosine, sine):
    half = values.shape[-1] // 2
    first = values[..., :half]
    second = values[..., half:]
    cosine = cosine[:, None, :]
    sine = sine[:, None, :]
    return jnp.concatenate(
        [first * cosine - second * sine, second * cosine + first * sine], axis=-1
    )


def rotate_back(grads, cosine, sine):
    half = grads.shape[-1] // 2
    first = grads[..., :half]
    second = grads[..., half:]
    cosine = cosine[:, None, :]
    sine = sine[:, None, :]
    return jnp.concatenate(
        [first * cosine + second * sine, second * cosine - first * sine], axis=-1
    )


def inverse(order, count):
    slots = jnp.arange(count, dtype=jnp.int32)
    matches = order[None, :] == slots[:, None]
    return jnp.sum(jnp.where(matches, slots[None, :], 0), axis=1)


def dot(left, right):
    return lax.dot_general(
        left, right, (((1,), (0,)), ((), ())), preferred_element_type=jnp.float32
    )


def dot_nt(left, right):
    return lax.dot_general(
        left, right, (((1,), (1,)), ((), ())), preferred_element_type=jnp.float32
    )


def dot_tn(left, right):
    return lax.dot_general(
        left, right, (((0,), (0,)), ((), ())), preferred_element_type=jnp.float32
    )


def swap(block):
    return lax.ppermute(block, "mp", [(0, 1), (1, 0)])


def cycle(block, axis, distance):
    count = lax.axis_size(axis)
    return lax.ppermute(block, axis, [(i, (i + distance) % count) for i in range(count)])


def tie(value, *others):
    return lax.optimization_barrier((value,) + others)[0]


def pick(blocks, index):
    return lax.dynamic_index_in_dim(blocks, index, 0, keepdims=False, allow_negative_indices=False)


def wrap(index, count):
    return index & (count - 1) if count & (count - 1) == 0 else lax.rem(index, count)


def gather_ctx(block):
    blocks = [block]
    for _ in range(lax.axis_size("ctx") - 1):
        blocks.append(cycle(blocks[-1], "ctx", 1))
    return blocks


def scatter_ctx(parts, steps=None):
    total = parts[1]
    for part in parts[2:] + parts[:1]:
        sent = total.astype(jnp.bfloat16)
        if steps is not None:
            steps.append(sent)
        arrived = cycle(sent, "ctx", 1)
        total = arrived.astype(jnp.float32) + part
    return total


def gather_ctx_direct(block):
    return [block] + [cycle(block, "ctx", s) for s in range(1, lax.axis_size("ctx"))]


def scatter_ctx_direct(parts):
    total = parts[0]
    for s in range(1, len(parts)):
        arrived = cycle(parts[s].astype(jnp.bfloat16), "ctx", -s)
        total = total + arrived.astype(jnp.float32)
    return total


def neighbour(block, bit):
    return lax.ppermute(block, "dp", [(i, i ^ bit) for i in range(4)])


def gather_dp(block):
    count = lax.axis_size("dp")
    rows, cols = block.shape
    if count != 4:
        return lax.all_gather(block, "dp", axis=0, tiled=True)
    half = rows // 2
    index = lax.axis_index("dp")
    along_x = neighbour(block, 1)
    along_y = neighbour(block, 2)
    far_first = neighbour(along_x[:half], 2)
    far_second = neighbour(along_y[half:], 1)
    whole = jnp.zeros((count, rows, cols), block.dtype)

    def place(whole, part, where, start):
        return lax.dynamic_update_slice(
            whole, part[None], (where, 0 * where + start, 0 * where), allow_negative_indices=False
        )

    whole = place(whole, block, index, 0)
    whole = place(whole, along_x, index ^ 1, 0)
    whole = place(whole, along_y, index ^ 2, 0)
    whole = place(whole, far_first, index ^ 3, 0)
    whole = place(whole, far_second, index ^ 3, half)
    return whole.reshape(count * rows, cols)


def scatter_dp(terms, *others):
    count = lax.axis_size("dp")
    rows, cols = terms.shape[0] // count, terms.shape[1]
    if count != 4:
        return lax.psum_scatter(terms, "dp", scatter_dimension=0, tiled=True).astype(jnp.float32)
    half = rows // 2
    index = lax.axis_index("dp")
    terms = terms.reshape(count, rows, cols)
    wide = lambda value: value.astype(jnp.float32)
    far = pick(terms, index ^ 3)
    from_x = neighbour(far[:half], 1)
    from_y = neighbour(far[half:], 2)
    to_x = wide(pick(terms, index ^ 1))
    to_y = wide(pick(terms, index ^ 2))
    if others:
        from_y = tie(from_y, *others)
        from_x = tie(from_x, *others)
    to_x = jnp.concatenate([to_x[:half], to_x[half:] + wide(from_y)]).astype(jnp.bfloat16)
    to_y = jnp.concatenate([to_y[:half] + wide(from_x), to_y[half:]]).astype(jnp.bfloat16)
    return wide(pick(terms, index)) + wide(neighbour(to_x, 1)) + wide(neighbour(to_y, 2))


def sum_all(block):
    block = block + swap(block)
    for axis in ("ctx", "dp"):
        count = lax.axis_size(axis)
        terms = jnp.stack([block] + [cycle(block, axis, s) for s in range(1, count)])
        index = lax.axis_index(axis)
        block = sum(pick(terms, wrap(index + count - j, count)) for j in range(count))
    return block


GROUPS = 3


def combine(weights, blocks):
    return sum(weights[k] * blocks[k].astype(jnp.float32) for k in range(len(blocks)))


def fold(block):
    tall = block.shape[0] // GROUPS
    return jnp.concatenate([block[g * tall : (g + 1) * tall] for g in range(GROUPS)], axis=1)


def unfold(block):
    wide = block.shape[1] // GROUPS
    return jnp.concatenate([block[:, g * wide : (g + 1) * wide] for g in range(GROUPS)], axis=0)


ATTEND_ROWS = 512


def seen_part(queries, keys, query_code, key_code, number):
    start = number * ATTEND_ROWS
    span = slice(start, start + ATTEND_ROWS + WINDOW)
    here = slice(start, start + ATTEND_ROWS)
    raw = dot_nt(queries[here], keys[span]) * HEAD_SIZE ** (-0.5)
    bent = jnp.tanh(raw * (1.0 / soft_cap))
    row = lax.broadcasted_iota(jnp.int32, raw.shape, 0)
    col = lax.broadcasted_iota(jnp.int32, raw.shape, 1)
    visible = (query_code[here] == key_code[:, span]) & (col > row) & (col <= row + WINDOW)
    visible = visible | (col == row + WINDOW)
    return here, span, jnp.where(visible, jnp.exp(soft_cap * bent), 0.0), bent


def attend_forward(queries, both, prev_both, query_code, key_code):
    joined = jnp.concatenate([prev_both, both], axis=0)
    keys, values = joined[:, :HEAD_SIZE], joined[:, HEAD_SIZE:]
    outs, sums = [], []
    for number in range(queries.shape[0] // ATTEND_ROWS):
        _, span, expo, _ = seen_part(queries, keys, query_code, key_code, number)
        total = jnp.sum(expo, axis=1, keepdims=True)
        outs.append(dot(expo.astype(jnp.bfloat16), values[span]) / total)
        sums.append(total)
    out = jnp.concatenate(outs, axis=0)
    return out.astype(jnp.bfloat16), out, jnp.concatenate(sums, axis=0)


def attend_backward(queries, both, prev_both, query_code, key_code, grads, full, sums):
    rows = queries.shape[0]
    scale = HEAD_SIZE ** (-0.5)
    joined = jnp.concatenate([prev_both, both], axis=0)
    keys, values = joined[:, :HEAD_SIZE], joined[:, HEAD_SIZE:]
    query_grads, pieces = [], []
    for number in range(rows // ATTEND_ROWS):
        here, span, expo, bent = seen_part(queries, keys, query_code, key_code, number)
        probs = expo * (1.0 / sums[here])
        prob_grad = dot_nt(grads[here], values[span])
        delta = jnp.sum(grads[here].astype(jnp.float32) * full[here], axis=1, keepdims=True)
        score = (probs * (prob_grad - delta) * (1.0 - bent * bent)).astype(jnp.bfloat16)
        query_grads.append(dot(score, keys[span]) * scale)
        part = jnp.concatenate(
            [dot_tn(score, queries[here]) * scale, dot_tn(probs.astype(jnp.bfloat16), grads[here])],
            axis=1,
        )
        pieces.append(jnp.pad(part, ((span.start, 2 * rows - span.stop), (0, 0))))
    total = sum(pieces)
    return (
        jnp.concatenate(query_grads, axis=0),
        total[rows:],
        total[:rows].astype(jnp.bfloat16),
    )


def body(
    tokens,
    cotangent,
    segments,
    padding,
    owners,
    gains,
    gain_stats,
    attention_input_master,
    attn_out,
    mlp_in,
    mlp_out,
    left_stats,
    right_stats,
    left_roots,
    right_roots,
):
    nctx = lax.axis_size("ctx")
    ctx_index = lax.axis_index("ctx")
    dp_index = lax.axis_index("dp")
    mp_index = lax.axis_index("mp")
    rows, width = tokens.shape
    half = rows // 2
    group_rows = rows * nctx
    dblock = attention_input_master.shape[0]
    key_columns = (attention_input_master.shape[1] - HEAD_SIZE) // 2
    ffn_cols = mlp_out.shape[1]
    piece = ffn_cols // nctx
    per_head = HEAD_SIZE // key_columns
    head_group = QUERY_HEADS // KEY_VALUE_HEADS
    before = lambda s: wrap(ctx_index + nctx - s, nctx)
    slots = jnp.arange(nctx, dtype=jnp.int32)
    one = lambda condition: condition.astype(jnp.float32)
    held = one(owners[:, None, :] == slots[None, :, None])
    turned_to = one(slots[None, :] == ((ctx_index + nctx - slots) % nctx)[:, None])
    my_query = jnp.sum(held[0] * turned_to[0][None, :], axis=1)
    key_weights, value_weights = [], []
    for part in range(per_head):
        wanted = one(slots[:, None] == (slots // head_group * per_head + part)[None, :])
        column = jnp.sum(wanted * my_query[None, :], axis=1)
        for row, weights in ((1, key_weights), (2, value_weights)):
            holder = jnp.sum(held[row] * column[:, None], axis=0)
            weights.append(jnp.sum(turned_to * holder[None, :], axis=1))
    paired = jnp.sum(held[0][:, :, None] * held[3][:, None, :], axis=0)
    paired_back = jnp.sum(paired[:, None, :] * turned_to[None, :, :], axis=2)

    def halves(block):
        pair = block.reshape((2, block.shape[0] // 2) + block.shape[1:])
        return jnp.where(mp_index == 0, pair, pair[::-1]).reshape(block.shape)

    def own_half(block):
        return lax.dynamic_slice_in_dim(block, mp_index * half, half, 0, allow_negative_indices=False)

    def other_half(block):
        return lax.dynamic_slice_in_dim(
            block, (1 - mp_index) * half, half, 0, allow_negative_indices=False
        )

    def both(block):
        return jnp.concatenate([block, swap(block)], axis=0)

    def in_order(blocks):
        stacked = jnp.stack(blocks)
        return jnp.concatenate([pick(stacked, before(j)) for j in range(nctx)], axis=0)

    def reduce_width(parts, steps=None):
        terms = []
        for part in parts:
            arrived = swap(part[half:].astype(jnp.bfloat16)).astype(jnp.float32)
            terms.append(part[:half] + arrived)
        return scatter_ctx(terms, steps)

    key_value = gather_ctx_direct(attention_input_master[:, HEAD_SIZE:].astype(jnp.bfloat16))
    low_in = [attention_input_master[:, :HEAD_SIZE]]
    for start, table in ((0, key_weights), (key_columns, value_weights)):
        parts = [block[:, start : start + key_columns] for block in key_value]
        low_in += [combine(weights, parts) for weights in table]
    whole_in = gather_dp(jnp.concatenate(low_in, axis=1).astype(jnp.bfloat16))

    def pass_on(block):
        return lax.all_to_all(block, "ctx", split_axis=0, concat_axis=0, tiled=True)

    def quarters_of(block):
        return [block[:, k * piece : (k + 1) * piece] for k in range(nctx)]

    def spread(master, column, row, *others):
        block = master if column is None else master[:, column[0] : column[0] + column[1]]
        dealt = jnp.stack([fold(quarter) for quarter in quarters_of(block.astype(jnp.bfloat16))])
        came = pass_on(tie(dealt, *others))
        blocks = [
            unfold(combine(held[row][b], [came[k] for k in range(nctx)]).astype(jnp.bfloat16))
            for b in range(nctx)
        ]
        return came, jnp.concatenate(blocks, axis=1)

    gate_came, low_gate = spread(mlp_in, (0, ffn_cols), 4, *key_value[1:])
    whole_gate = gather_dp(low_gate)
    out_blocks = gather_ctx_direct(tie(attn_out.astype(jnp.bfloat16), gate_came))
    whole_out = gather_dp(
        jnp.concatenate([combine(paired_back[j], out_blocks) for j in range(nctx)], axis=1).astype(
            jnp.bfloat16
        )
    )

    inputs = own_half(tokens).astype(jnp.float32)
    first_out, first_normed, first_scale = normalize(inputs, gains[0])
    first_blocks = gather_ctx(tie(first_out.astype(jnp.bfloat16), out_blocks[2]))
    hidden_in = [both(block) for block in first_blocks]
    _, low_up = spread(mlp_in, (ffn_cols, ffn_cols), 5, first_blocks[3])
    whole_up = gather_dp(low_up)
    _, low_down = spread(mlp_out, None, 6, first_blocks[3])
    whole_down = gather_dp(low_down)
    projected = in_order([halves(dot(block, whole_in)) for block in hidden_in])
    group_first = dp_index * group_rows
    group_pos = group_first + jnp.arange(group_rows, dtype=jnp.int32)
    cosine, sine = rotation(group_pos % PACKED_TOKENS)
    turned = rotate(
        projected[:, : 2 * HEAD_SIZE].reshape(group_rows, 2, HEAD_SIZE), cosine, sine
    ).astype(jnp.bfloat16)
    queries_h = turned[:, 0]
    both_h = jnp.concatenate(
        [turned[:, 1], projected[:, 2 * HEAD_SIZE :].astype(jnp.bfloat16)], axis=1
    )
    prev_both = shifted(both_h, "dp", 1)
    codes = segments + PACKED_TOKENS * (
        jnp.arange(segments.shape[0], dtype=jnp.int32) // PACKED_TOKENS
    )
    nobody = jnp.full((group_rows,), -1, jnp.int32)
    key_codes = jnp.concatenate([nobody, jnp.where(padding == 1, codes, -1)])
    key_code = lax.dynamic_slice_in_dim(
        key_codes, group_first, 2 * group_rows, 0, allow_negative_indices=False
    )[None, :]
    query_code = lax.dynamic_slice_in_dim(
        codes, group_first, group_rows, 0, allow_negative_indices=False
    )[:, None]
    attended_low, attended, prob_sums = attend_forward(
        tie(queries_h, low_up), both_h, prev_both, query_code, key_code
    )
    came = pass_on(attended_low.reshape(nctx, rows, HEAD_SIZE))
    heads_out = jnp.concatenate([came[j] for j in range(nctx)], axis=1)
    attn_part = dot_nt(tie(heads_out, low_down), whole_out)
    attn = own_half(attn_part) + swap(other_half(attn_part).astype(jnp.bfloat16)).astype(
        jnp.float32
    )
    second_out, second_normed, second_scale = normalize(attn, gains[1])
    mixed = inputs + second_out
    third_out, third_normed, third_scale = normalize(mixed, gains[2])

    hidden_two = [both(block) for block in gather_ctx(third_out.astype(jnp.bfloat16))]
    pulls, actives, uppers, gelus, moved_parts = [], [], [], [], []
    for block in hidden_two:
        gate = dot(block, whole_gate)
        upper = dot(block, whole_up)
        gelu_value, gelu_pull = jax.vjp(lambda values: jax.nn.gelu(values, approximate=True), gate)
        active = (gelu_value * upper).astype(jnp.bfloat16)
        pulls.append(gelu_pull)
        actives.append(active)
        uppers.append(upper)
        gelus.append(gelu_value)
        moved_parts.append(dot_nt(active, whole_down))
    moved = reduce_width(moved_parts)
    fourth_out, fourth_normed, fourth_scale = normalize(moved, gains[3])
    block_out = halves(both((mixed + fourth_out).astype(jnp.bfloat16)))
    upstream = own_half(cotangent).astype(jnp.float32)
    moved_grad, fourth_gain = norm_back(fourth_normed, fourth_scale, gains[3], upstream)
    moved_low = [both(block) for block in gather_ctx(moved_grad.astype(jnp.bfloat16))]
    gate_grads, upper_grads, hidden_two_parts = [], [], []
    for s, block in enumerate(moved_low):
        active_grad = dot(block, whole_down)
        gate_grad = pulls[s](active_grad * uppers[s])[0].astype(jnp.bfloat16)
        upper_grad = (active_grad * gelus[s]).astype(jnp.bfloat16)
        gate_grads.append(gate_grad)
        upper_grads.append(upper_grad)
        hidden_two_parts.append(dot_nt(gate_grad, whole_gate) + dot_nt(upper_grad, whole_up))
    steps = []
    hidden_two_grad = reduce_width(hidden_two_parts, steps)
    cat = lambda values: jnp.concatenate(values, axis=0)
    low = lambda values: values.astype(jnp.bfloat16)
    down_terms = low(dot_tn(cat(moved_low), cat(actives)))
    hidden_two_all = cat(hidden_two)
    gate_terms = low(dot_tn(hidden_two_all, tie(cat(gate_grads), steps[1])))
    up_terms = low(dot_tn(hidden_two_all, tie(cat(upper_grads), steps[2])))
    down_sum = scatter_dp(down_terms)
    gate_sum = scatter_dp(gate_terms)

    def collect(summed, row):
        quarters = quarters_of(summed)
        dealt = [fold(low(combine(held[row][:, k], quarters))) for k in range(nctx)]
        came = pass_on(jnp.stack(dealt))
        return came, jnp.concatenate([unfold(came[j]) for j in range(nctx)], axis=1).astype(
            jnp.float32
        )

    mixed_part, third_gain = norm_back(third_normed, third_scale, gains[2], hidden_two_grad)
    mixed_grad = upstream + mixed_part
    attn_grad, second_gain = norm_back(second_normed, second_scale, gains[1], mixed_grad)
    attn_low = halves(both(attn_grad.astype(jnp.bfloat16)))
    heads_grad = low(dot(attn_low, whole_out))

    head_grad = pass_on(
        jnp.stack([heads_grad[:, j * HEAD_SIZE : (j + 1) * HEAD_SIZE] for j in range(nctx)])
    ).reshape(group_rows, HEAD_SIZE)

    query_grads, both_own, both_prev = attend_backward(
        queries_h, both_h, prev_both, query_code, key_code, head_grad, attended, prob_sums
    )
    both_next = shifted(both_prev, "dp", -1)
    up_sum = scatter_dp(up_terms, both_next)
    down_came, down_grad = collect(tie(down_sum, head_grad), 6)
    gate_came, gate_grad_whole = collect(tie(gate_sum, down_came), 4)
    up_came, up_grad_whole = collect(tie(up_sum, gate_came), 5)
    both_total = both_own + both_next.astype(jnp.float32)
    turned_back = rotate_back(
        jnp.stack([query_grads, both_total[:, :HEAD_SIZE]], axis=1), cosine, sine
    ).reshape(group_rows, 2 * HEAD_SIZE)
    right_attn = low(jnp.concatenate([turned_back, both_total[:, HEAD_SIZE:]], axis=1)).reshape(
        nctx, rows, 3 * HEAD_SIZE
    )
    right_attn = cat([halves(pick(right_attn, before(s))) for s in range(nctx)])
    parts = [dot_nt(right_attn[s * rows : (s + 1) * rows], whole_in) for s in range(nctx)]
    terms = [part[:half] + swap(low(part[half:])).astype(jnp.float32) for part in parts]
    sent_one = low(terms[1])
    sent_two = low(cycle(sent_one, "ctx", 1).astype(jnp.float32) + terms[2])
    sent_two = tie(sent_two, gate_came)
    sent_three = low(cycle(sent_two, "ctx", 1).astype(jnp.float32) + terms[3])
    hidden_grad = cycle(sent_three, "ctx", 1).astype(jnp.float32) + terms[0]
    input_part, first_gain = norm_back(first_normed, first_scale, gains[0], hidden_grad)
    input_grad = halves(both(mixed_grad + input_part))

    out_sum = scatter_dp(low(dot_tn(tie(attn_low, sent_one), heads_out)))
    in_terms = low(dot_tn(cat(hidden_in), tie(right_attn, sent_one)))
    in_sum = scatter_dp(in_terms)
    heads = [out_sum[:, j * HEAD_SIZE : (j + 1) * HEAD_SIZE] for j in range(nctx)]
    heads[0] = tie(heads[0], up_came)
    out_grad = scatter_ctx_direct([combine(paired_back[:, s], heads) for s in range(nctx)])
    sums = [
        in_sum[:, start + p * key_columns : start + (p + 1) * key_columns]
        for start in (HEAD_SIZE, 2 * HEAD_SIZE)
        for p in range(per_head)
    ]
    key_value_grad = scatter_ctx_direct(
        [
            jnp.concatenate(
                [
                    sum(weights[s] * block for weights, block in zip(table, blocks))
                    for table, blocks in (
                        (key_weights, sums[:per_head]),
                        (value_weights, sums[per_head:]),
                    )
                ],
                axis=1,
            )
            for s in range(nctx)
        ]
    )
    grad_attn_in = jnp.concatenate([in_sum[:, :HEAD_SIZE], key_value_grad], axis=1)
    grad_mlp_in = jnp.concatenate([gate_grad_whole, up_grad_whole], axis=1)

    gain_grad = sum_all(jnp.stack([first_gain, second_gain, third_gain, fourth_gain], axis=0))
    new_gain_stats = stat_decay * gain_stats + (1.0 - stat_decay) * gain_grad * gain_grad
    new_gains = gains - gain_rate * gain_grad * lax.rsqrt(new_gain_stats)

    stats = tuple(
        value.reshape(value.shape[3:])
        for value in (left_stats, right_stats, left_roots, right_roots)
    )
    in_blocks = attention_input_master.shape[1] // SUBW
    out_count = attn_out.shape[1] // SUBW
    ffn_blocks = ffn_cols // SUBW
    first = in_blocks + out_count
    masters = (attention_input_master, attn_out, mlp_in, mlp_out)
    grads = (grad_attn_in, out_grad, grad_mlp_in, down_grad)
    pieces = [
        jnp.transpose(grad.reshape(dblock, grad.shape[1] // SUBW, SUBW), (1, 0, 2))
        for grad in grads
    ]
    stacked = low(jnp.concatenate(pieces, axis=0))
    batched = lambda left, right, sum_left, sum_right: lax.dot_general(
        left, right, (((sum_left,), (sum_right,)), ((0,), (0,))), preferred_element_type=jnp.float32
    )
    new_left = stat_decay * stats[0] + (1.0 - stat_decay) * batched(stacked, stacked, 2, 2)
    new_right = stat_decay * stats[1] + (1.0 - stat_decay) * batched(stacked, stacked, 1, 1)
    step = batched(low(batched(low(stats[2]), stacked, 2, 1)), low(stats[3]), 2, 1)
    updated = []
    offset = 0
    for master in masters:
        count = master.shape[1] // SUBW
        part = jnp.transpose(step[offset : offset + count], (1, 0, 2))
        updated.append(master - master_rate * part.reshape(dblock, master.shape[1]))
        offset = offset + count
    new_attn_in, new_attn_out, new_mlp_in, new_mlp_out = updated
    return (
        block_out,
        input_grad,
        grad_attn_in,
        out_grad,
        grad_mlp_in,
        down_grad,
        new_attn_in,
        new_attn_out,
        new_mlp_in,
        new_mlp_out,
        new_left.reshape(left_stats.shape),
        new_right.reshape(right_stats.shape),
        gain_grad,
        new_gain_stats,
        new_gains,
    )


def solution(mesh):
    return jax.shard_map(
        body,
        mesh=mesh,
        in_specs=(
            P(("dp", "ctx"), None),
            P(("dp", "ctx"), None),
            P(),
            P(),
            P(),
            P(),
            P(),
            P("dp", ("ctx", "mp")),
            P("dp", ("ctx", "mp")),
            P("dp", ("ctx", "mp")),
            P("dp", ("ctx", "mp")),
            P("dp", "ctx", "mp", None, None, None),
            P("dp", "ctx", "mp", None, None, None),
            P("dp", "ctx", "mp", None, None, None),
            P("dp", "ctx", "mp", None, None, None),
        ),
        out_specs=(
            P(("dp", "ctx"), None),
            P(("dp", "ctx"), None),
            P("dp", ("ctx", "mp")),
            P("dp", ("ctx", "mp")),
            P("dp", ("ctx", "mp")),
            P("dp", ("ctx", "mp")),
            P("dp", ("ctx", "mp")),
            P("dp", ("ctx", "mp")),
            P("dp", ("ctx", "mp")),
            P("dp", ("ctx", "mp")),
            P("dp", "ctx", "mp", None, None, None),
            P("dp", "ctx", "mp", None, None, None),
            P(),
            P(),
            P(),
        ),
        check_vma=False,
    )
```

time: 3800 us -> 1170 us (0.31)
  waiting for transfers between devices: 2740 us -> 269 us
  starting transfers between devices: 39.6 us -> 182 us
  local copies, waits for them, and re-layouts: 332 us -> 203 us
  blocking collectives: 108 us -> 0 us
  matrix products: 326 us -> 224 us
  other arithmetic: 219 us -> 274 us
    reduce_scatter x2 -> x0, waiting for transfers between devices: 1890 us -> none  [the longest x1 1810 us: body(): lax.psum_scatter(pair_terms(((hidden_two, right_mlp), (moved_low, active_...]
    all_gather x4 -> x0, waiting for transfers between devices: 770 us -> none  [the longest x1 421 us: body(): lax.all_gather(mlp_in_low, ('dp', 'ctx'), axis=0, tiled=True)]
    ppermute x0 -> x105, waiting for transfers between devices: none -> 215 us  [the longest x36 150 us: cycle(): lax.ppermute(block, axis, [(i, (i + distance) % count) for i in range(cou...]
    ppermute x0 -> x105, starting transfers between devices: none -> 129 us  [the longest x36 80.1 us: cycle(): lax.ppermute(block, axis, [(i, (i + distance) % count) for i in range(cou...]
    transpose x6 -> x0, local copies, waits for them, and re-layouts: 102 us -> none  [the longest x4 102 us: pair_term(): jnp.einsum('tdr,tcw->dcrw', columns, right, preferred_element_type=jnp.fl...]
    dot_general x32 -> x56, matrix products: 326 us -> 224 us  [the longest x23 65.9 us: dot_nt(): lax.dot_general(left, right, (((1,), (1,)), ((), ())), preferred_element_...]
    psum x1 -> x0, blocking collectives: 82.3 us -> none  [body(): lax.psum(jnp.stack([first_gain, second_gain, third_gain, fourth_gain], ax...]
    concatenate x6 -> x56, other arithmetic: 103 us -> 41.7 us  [the longest x24 12.6 us: unfold(): jnp.concatenate([block[:, g * wide:(g + 1) * wide] for g in range(GROUPS)...]
  transfers between devices with their start and end apart: 21 -> 115, of which waited for: 13 -> 41; matrix products, arithmetic and copies ran while one was open for 12% -> 55% of each run, Pallas kernels for 0% -> 0%
where the time goes in v1:
time: 1170 us; the launch traced here: 1160 us
  other arithmetic  274 us (23%)
  waiting for transfers between devices  269 us (23%)
  matrix products  224 us (19%)
  local copies, waits for them, and re-layouts  203 us (17%)
  starting transfers between devices  182 us (16%)
    ppermute x36, waiting for transfers between devices, cycle(): lax.ppermute(block, axis, [(i, (i + distance) % count) for i in range(cou...  150 us
    ppermute x36, starting transfers between devices, cycle(): lax.ppermute(block, axis, [(i, (i + distance) % count) for i in range(cou...  80.1 us
    dot_general x23, matrix products, dot_nt(): lax.dot_general(left, right, (((1,), (1,)), ((), ())), preferred_element_...  65.9 us
    ppermute x40, waiting for transfers between devices, neighbour(): return lax.ppermute(block, 'dp', [(i, i ^ bit) for i in range(4)])  63.1 us
    dot_general x3, matrix products, body(): lax.dot_general(left, right, (((sum_left,), (sum_right,)), ((0,), (0,))),...  62.5 us
    unnamed x353, local copies, waits for them, and re-layouts  60.1 us
    dot_general x21, matrix products, dot(): lax.dot_general(left, right, (((1,), (0,)), ((), ())), preferred_element_...  59.3 us
    all_to_all x8, starting transfers between devices, pass_on(): return lax.all_to_all(block, 'ctx', split_axis=0, concat_axis=0, tiled=True)  47.6 us
  transfers between devices with their start and end apart: 115, of which 41 were waited for; matrix products, arithmetic and copies ran while one was open for 55% of the time, Pallas kernels for 0%

profile of v1, /device:TPU:0, one launch (start us, length us, event | category | flops | bytes accessed | tf_op | source)
XLA Modules:
  0.0 1157.7 jit_solution(644283468931222933)
XLA Ops:
  77.8 15.0 %all-to-all-start = ((bf16[4,192,864]{2,1,0:T(8,128)(2,1)}), bf16[4,192,864]{2,1,0:T(8,128)(2,1)}, u32[]{:S(2)}, u32[]{:S(2)}) async-start(bf16[4,192,864]{2,1,0:T(8,128)(2,1)} %pad_maximum_fusion.7), calls=%async_computation | async-start | bytes 2752512 | tf_op jit(solution)/shard_map/all_to_all | solution.py:361
  110.0 14.2 %all-to-all-done = bf16[4,192,864]{2,1,0:T(8,128)(2,1)} async-done(((bf16[4,192,864]{2,1,0:T(8,128)(2,1)}), bf16[4,192,864]{2,1,0:T(8,128)(2,1)}, u32[]{:S(2)}, u32[]{:S(2)}) %all-to-all-start) | async-done | bytes 1327136 | tf_op jit(solution)/shard_map/all_to_all | solution.py:361
  124.2 6.6 fusion.252
  130.9 6.7 fusion.253
  153.9 11.2 collective-permute-done.3
  170.3 8.1 fusion.228
  186.5 16.5 %collective-permute-start.11 = (bf16[128,2304]{1,0:T(8,128)(2,1)S(1)}, bf16[128,2304]{1,0:T(8,128)(2,1)}, u32[]{:S(2)}, u32[]{:S(2)}) collective-permute-start(bf16[128,2304]{1,0:T(8,128)(2,1)S(1)} %collective-permute-done.9), channel_id=1, source_target_pairs={{0,2},{2,4},{4,6},{6,0},{1,3},{3,5},{5,7},{7,1},{8,10},{10,12},{12... | collective-permute-start | bytes 1769480 | tf_op jit(solution)/shard_map/ppermute | solution.py:102
  215.2 18.0 %collective-permute-start.13 = (bf16[128,2304]{1,0:T(8,128)(2,1)}, bf16[128,2304]{1,0:T(8,128)(2,1)}, u32[]{:S(2)}, u32[]{:S(2)}) collective-permute-start(bf16[128,2304]{1,0:T(8,128)(2,1)} %collective-permute-done.11), channel_id=1, source_target_pairs={{0,2},{2,4},{4,6},{6,0},{1,3},{3,5},{5,7},{7,1},{8,10},{10,12},{12... | collective-permute-start | bytes 1769480 | tf_op jit(solution)/shard_map/ppermute | solution.py:102
  293.0 6.6 fusion.260
  299.9 6.6 fusion.261
  359.4 6.8 all-to-all-done.2
  391.3 8.0 collective-permute-done.23
  414.8 6.5 collective-permute-done.39
  468.8 9.7 collective-permute-done.42
  481.9 12.7 %collective-permute-done.46 = bf16[128,2304]{1,0:T(8,128)(2,1)S(1)} collective-permute-done((bf16[128,2304]{1,0:T(8,128)(2,1)S(1)}, bf16[128,2304]{1,0:T(8,128)(2,1)S(1)}, u32[]{:S(2)}, u32[]{:S(2)}) %collective-permute-start.46) | collective-permute-done | bytes 589856 | tf_op jit(solution)/shard_map/ppermute | solution.py:102
  565.8 6.7 convolution_convert_fusion.2
  575.9 8.2 convolution_convert_fusion.1
  589.4 8.2 convolution_convert_fusion
  608.1 9.2 collective-permute-done.61
  635.4 40.5 %collective-permute-done.76 = bf16[576,1152]{1,0:T(8,128)(2,1)} collective-permute-done((bf16[576,1152]{1,0:T(8,128)(2,1)}, bf16[576,1152]{1,0:T(8,128)(2,1)}, u32[]{:S(2)}, u32[]{:S(2)}) %collective-permute-start.76) | collective-permute-done | bytes 1327136 | tf_op jit(solution)/shard_map/ppermute | solution.py:148
  722.7 19.8 %collective-permute-done.65 = bf16[1024,512]{1,0:T(8,128)(2,1)S(1)} collective-permute-done((bf16[1024,512]{1,0:T(8,128)(2,1)S(1)}, bf16[1024,512]{1,0:T(8,128)(2,1)S(1)}, u32[]{:S(2)}, u32[]{:S(2)}) %collective-permute-start.65) | collective-permute-done | bytes 1048608 | tf_op jit(solution)/shard_map/ppermute | solution.py:28
  783.9 6.9 convolution_convert_fusion.4
  824.2 25.6 %collective-permute-done.67 = bf16[128,2304]{1,0:T(8,128)(2,1)S(1)} collective-permute-done((bf16[128,2304]{1,0:T(8,128)(2,1)}, bf16[128,2304]{1,0:T(8,128)(2,1)S(1)}, u32[]{:S(2)}, u32[]{:S(2)}) %collective-permute-start.67) | collective-permute-done | bytes 589856 | tf_op jit(solution)/shard_map/ppermute | solution.py:102
  853.4 11.9 %collective-permute-done.85 = bf16[576,768]{1,0:T(8,128)(2,1)S(1)} collective-permute-done((bf16[576,768]{1,0:T(8,128)(2,1)S(1)}, bf16[576,768]{1,0:T(8,128)(2,1)S(1)}, u32[]{:S(2)}, u32[]{:S(2)}) %collective-permute-start.85) | collective-permute-done | bytes 884768 | tf_op jit(solution)/shard_map/ppermute | solution.py:148
  891.7 9.5 collective-permute-done.87
  907.8 6.8 collective-permute-start.77
  947.6 24.5 %collective-permute-done.79 = bf16[128,2304]{1,0:T(8,128)(2,1)} collective-permute-done((bf16[128,2304]{1,0:T(8,128)(2,1)}, bf16[128,2304]{1,0:T(8,128)(2,1)}, u32[]{:S(2)}, u32[]{:S(2)}) %collective-permute-start.79) | collective-permute-done | bytes 589856 | tf_op jit(solution)/shard_map/ppermute | solution.py:102
  978.3 6.6 collective-permute-start.102
  999.2 7.1 add_convert_fusion.17
  1046.8 23.7 %fusion.6 = f32[33,576,128]{2,1,0:T(8,128)} fusion(f32[1,1,1,33,576,576]{5,4,3,2,1,0:T(8,128)} %param.28, f32[1,1,1,33,128,128]{5,4,3,2,1,0:T(8,128)} %param.29, bf16[9,576,128]{2,1,0:T(8,128)(2,1)} %bitcast.668, bf16[18,576,128]{2,1,0:T(8,128)(2,1)} %maximum_bitcast_fusion, bf16[2,576,128]{2,1,0:T(8,128)(2,1)S(1)} %bitcast.716, ...), kind=kOutput, calls=%fused_computation.15 | convolution fusion | flops 3459084288 | bytes 60555264 | tf_op jit(solution)/shard_map/dot_general | solution.py:558
  1085.7 7.6 bitcast_subtract_fusion
  1110.5 35.1 %fusion.1 = f32[1,1,1,33,576,576]{5,4,3,2,1,0:T(8,128)} fusion(f32[1,1,1,33,576,576]{5,4,3,2,1,0:T(8,128)} %param.26, bf16[9,576,128]{2,1,0:T(8,128)(2,1)} %bitcast.669, bf16[18,576,128]{2,1,0:T(8,128)(2,1)S(1)} %copy-done.5, bf16[2,576,128]{2,1,0:T(8,128)(2,1)S(1)} %bitcast.717, bf16[4,576,128]{2,1,0:T(8,128)(2,1)S(1)} %bitcast.678), kind=kOutput, calls=%fused_computation.2 | convolution fusion | flops 2832039936 | bytes 92454912 | tf_op jit(solution)/shard_map/dot_general | solution.py:558
  (972 shorter events, 742.1 us)
Async XLA Ops:
  2.7 55.0 %collective-permute-start = (bf16[576,256]{1,0:T(8,128)(2,1)}, bf16[576,256]{1,0:T(8,128)(2,1)S(1)}, u32[]{:S(2)}, u32[]{:S(2)}) collective-permute-start(bf16[576,256]{1,0:T(8,128)(2,1)} %slice.2503), channel_id=1, source_target_pairs={{0,2},{2,4},{4,6},{6,0},{1,3},{3,5},{5,7},{7,1},{8,10},{10,12},{12... | collective-permute-start | bytes 884744 | tf_op jit(solution)/shard_map/ppermute | solution.py:102
  5.8 52.0 %collective-permute-start.1 = (bf16[576,256]{1,0:T(8,128)(2,1)}, bf16[576,256]{1,0:T(8,128)(2,1)}, u32[]{:S(2)}, u32[]{:S(2)}) collective-permute-start(bf16[576,256]{1,0:T(8,128)(2,1)} %slice.2503), channel_id=1, source_target_pairs={{0,4},{2,6},{4,0},{6,2},{1,5},{3,7},{5,1},{7,3},{8,12},{10,14},{12... | collective-permute-start | bytes 884744 | tf_op jit(solution)/shard_map/ppermute | solution.py:102
  8.3 49.4 %collective-permute-start.2 = (bf16[576,256]{1,0:T(8,128)(2,1)}, bf16[576,256]{1,0:T(8,128)(2,1)}, u32[]{:S(2)}, u32[]{:S(2)}) collective-permute-start(bf16[576,256]{1,0:T(8,128)(2,1)} %slice.2503), channel_id=1, source_target_pairs={{0,6},{2,0},{4,2},{6,4},{1,7},{3,1},{5,3},{7,5},{8,14},{10,8},{12,... | collective-permute-start | bytes 884744 | tf_op jit(solution)/shard_map/ppermute | solution.py:102
  77.8 46.3 %all-to-all-start = ((bf16[4,192,864]{2,1,0:T(8,128)(2,1)}), bf16[4,192,864]{2,1,0:T(8,128)(2,1)}, u32[]{:S(2)}, u32[]{:S(2)}) async-start(bf16[4,192,864]{2,1,0:T(8,128)(2,1)} %pad_maximum_fusion.7), calls=%async_computation | async-start | bytes 2752512 | tf_op jit(solution)/shard_map/all_to_all | solution.py:361
  145.1 61.7 %collective-permute-start.25 = (bf16[576,1152]{1,0:T(8,128)(2,1)}, bf16[576,1152]{1,0:T(8,128)(2,1)S(1)}, u32[]{:S(2)}, u32[]{:S(2)}) collective-permute-start(bf16[576,1152]{1,0:T(8,128)(2,1)} %concatenate.447), channel_id=1, source_target_pairs={{0,8},{8,0},{16,24},{24,16},{1,9},{9,1},{17,25},{25,17},{2,10},{10... | collective-permute-start | bytes 3981320 | tf_op jit(solution)/shard_map/ppermute | solution.py:148
  145.6 62.4 %collective-permute-start.26 = (bf16[576,1152]{1,0:T(8,128)(2,1)}, bf16[576,1152]{1,0:T(8,128)(2,1)S(1)}, u32[]{:S(2)}, u32[]{:S(2)}) collective-permute-start(bf16[576,1152]{1,0:T(8,128)(2,1)} %concatenate.447), channel_id=1, source_target_pairs={{0,16},{8,24},{16,0},{24,8},{1,17},{9,25},{17,1},{25,9},{2,18},{10... | collective-permute-start | bytes 3981320 | tf_op jit(solution)/shard_map/ppermute | solution.py:148
  214.7 53.5 %collective-permute-start.21 = (bf16[288,1024]{1,0:T(8,128)(2,1)}, bf16[288,1024]{1,0:T(8,128)(2,1)}, u32[]{:S(2)}, u32[]{:S(2)}) collective-permute-start(bf16[288,1024]{1,0:T(8,128)(2,1)} %slice.2624), channel_id=1, source_target_pairs={{0,8},{8,0},{16,24},{24,16},{1,9},{9,1},{17,25},{25,17},{2,10},{10... | collective-permute-start | bytes 1769480 | tf_op jit(solution)/shard_map/ppermute | solution.py:148
  242.4 38.8 %all-to-all-start.1 = ((bf16[4,192,864]{2,1,0:T(8,128)(2,1)}), bf16[4,192,864]{2,1,0:T(8,128)(2,1)}, u32[]{:S(2)}, u32[]{:S(2)}) async-start(bf16[4,192,864]{2,1,0:T(8,128)(2,1)} %pad_maximum_fusion.8), calls=%async_computation.1 | async-start | bytes 2752512 | tf_op jit(solution)/shard_map/all_to_all | solution.py:361
  312.1 60.1 %collective-permute-start.29 = (bf16[576,1152]{1,0:T(8,128)(2,1)}, bf16[576,1152]{1,0:T(8,128)(2,1)}, u32[]{:S(2)}, u32[]{:S(2)}) collective-permute-start(bf16[576,1152]{1,0:T(8,128)(2,1)} %concatenate.422), channel_id=1, source_target_pairs={{0,8},{8,0},{16,24},{24,16},{1,9},{9,1},{17,25},{25,17},{2,10},{10... | collective-permute-start | bytes 3981320 | tf_op jit(solution)/shard_map/ppermute | solution.py:148
  314.6 59.5 %collective-permute-start.30 = (bf16[576,1152]{1,0:T(8,128)(2,1)}, bf16[576,1152]{1,0:T(8,128)(2,1)}, u32[]{:S(2)}, u32[]{:S(2)}) collective-permute-start(bf16[576,1152]{1,0:T(8,128)(2,1)} %concatenate.422), channel_id=1, source_target_pairs={{0,16},{8,24},{16,0},{24,8},{1,17},{9,25},{17,1},{25,9},{2,18},{10... | collective-permute-start | bytes 3981320 | tf_op jit(solution)/shard_map/ppermute | solution.py:148
  337.0 44.8 %collective-permute-start.33 = (bf16[576,1152]{1,0:T(8,128)(2,1)}, bf16[576,1152]{1,0:T(8,128)(2,1)}, u32[]{:S(2)}, u32[]{:S(2)}) collective-permute-start(bf16[576,1152]{1,0:T(8,128)(2,1)} %concatenate.435), channel_id=1, source_target_pairs={{0,8},{8,0},{16,24},{24,16},{1,9},{9,1},{17,25},{25,17},{2,10},{10... | collective-permute-start | bytes 3981320 | tf_op jit(solution)/shard_map/ppermute | solution.py:148
  337.6 48.0 %collective-permute-start.34 = (bf16[576,1152]{1,0:T(8,128)(2,1)}, bf16[576,1152]{1,0:T(8,128)(2,1)}, u32[]{:S(2)}, u32[]{:S(2)}) collective-permute-start(bf16[576,1152]{1,0:T(8,128)(2,1)} %concatenate.435), channel_id=1, source_target_pairs={{0,16},{8,24},{16,0},{24,8},{1,17},{9,25},{17,1},{25,9},{2,18},{10... | collective-permute-start | bytes 3981320 | tf_op jit(solution)/shard_map/ppermute | solution.py:148
  511.8 96.3 %collective-permute-start.63 = (bf16[128,2304]{1,0:T(8,128)(2,1)}, bf16[128,2304]{1,0:T(8,128)(2,1)S(1)}, u32[]{:S(2)}, u32[]{:S(2)}) collective-permute-start(bf16[128,2304]{1,0:T(8,128)(2,1)} %slice.3154), channel_id=1, source_target_pairs={{0,1},{1,0},{2,3},{3,2},{4,5},{5,4},{6,7},{7,6},{8,9},{9,8},{10,11... | collective-permute-start | bytes 1769480 | tf_op jit(solution)/shard_map/ppermute | solution.py:97
  602.7 156.8 %collective-permute-start.93 = (bf16[288,1152]{1,0:T(8,128)(2,1)}, bf16[288,1152]{1,0:T(8,128)(2,1)}, u32[]{:S(2)}, u32[]{:S(2)}) collective-permute-start(bf16[288,1152]{1,0:T(8,128)(2,1)} %get-tuple-element.132), channel_id=1, source_target_pairs={{0,16},{8,24},{16,0},{24,8},{1,17},{9,25},{17,1},{25,9},{2,18},{10... | collective-permute-start | bytes 1990664 | tf_op jit(solution)/shard_map/ppermute | solution.py:148
  605.6 153.9 %collective-permute-start.95 = (bf16[288,1152]{1,0:T(8,128)(2,1)}, bf16[288,1152]{1,0:T(8,128)(2,1)}, u32[]{:S(2)}, u32[]{:S(2)}) collective-permute-start(bf16[288,1152]{1,0:T(8,128)(2,1)} %get-tuple-element.134), channel_id=1, source_target_pairs={{0,8},{8,0},{16,24},{24,16},{1,9},{9,1},{17,25},{25,17},{2,10},{10... | collective-permute-start | bytes 1990664 | tf_op jit(solution)/shard_map/ppermute | solution.py:148
  606.2 112.6 %collective-permute-start.72 = (bf16[576,1152]{1,0:T(8,128)(2,1)}, bf16[576,1152]{1,0:T(8,128)(2,1)}, u32[]{:S(2)}, u32[]{:S(2)}) collective-permute-start(bf16[576,1152]{1,0:T(8,128)(2,1)} %pad_maximum_fusion.14), channel_id=1, source_target_pairs={{0,16},{8,24},{16,0},{24,8},{1,17},{9,25},{17,1},{25,9},{2,18},{10... | collective-permute-start | bytes 3981320 | tf_op jit(solution)/shard_map/ppermute | solution.py:148
  620.2 55.6 %collective-permute-start.76 = (bf16[576,1152]{1,0:T(8,128)(2,1)}, bf16[576,1152]{1,0:T(8,128)(2,1)}, u32[]{:S(2)}, u32[]{:S(2)}) collective-permute-start(bf16[576,1152]{1,0:T(8,128)(2,1)} %pad_maximum_fusion.16), channel_id=1, source_target_pairs={{0,16},{8,24},{16,0},{24,8},{1,17},{9,25},{17,1},{25,9},{2,18},{10... | collective-permute-start | bytes 3981320 | tf_op jit(solution)/shard_map/ppermute | solution.py:148
  624.6 52.7 %collective-permute-start.74 = (bf16[576,1152]{1,0:T(8,128)(2,1)}, bf16[576,1152]{1,0:T(8,128)(2,1)}, u32[]{:S(2)}, u32[]{:S(2)}) collective-permute-start(bf16[576,1152]{1,0:T(8,128)(2,1)} %pad_maximum_fusion.15), channel_id=1, source_target_pairs={{0,8},{8,0},{16,24},{24,16},{1,9},{9,1},{17,25},{25,17},{2,10},{10... | collective-permute-start | bytes 3981320 | tf_op jit(solution)/shard_map/ppermute | solution.py:148
  631.2 62.7 %all-to-all-start.4 = ((bf16[4,256,256]{2,1,0:T(8,128)(2,1)}), bf16[4,256,256]{2,1,0:T(8,128)(2,1)}, u32[]{:S(2)}, u32[]{:S(2)}) async-start(bf16[4,256,256]{2,1,0:T(8,128)(2,1)} %pad_maximum_fusion.39), calls=%async_computation.4 | async-start | bytes 1048576 | tf_op jit(solution)/shard_map/all_to_all | solution.py:361
  675.8 43.0 %collective-permute-start.70 = (bf16[576,1152]{1,0:T(8,128)(2,1)}, bf16[576,1152]{1,0:T(8,128)(2,1)}, u32[]{:S(2)}, u32[]{:S(2)}) collective-permute-start(bf16[576,1152]{1,0:T(8,128)(2,1)} %pad_maximum_fusion.13), channel_id=1, source_target_pairs={{0,8},{8,0},{16,24},{24,16},{1,9},{9,1},{17,25},{25,17},{2,10},{10... | collective-permute-start | bytes 3981320 | tf_op jit(solution)/shard_map/ppermute | solution.py:148
  693.9 71.4 %all-to-all-start.5 = ((bf16[4,192,864]{2,1,0:T(8,128)(2,1)}), bf16[4,192,864]{2,1,0:T(8,128)(2,1)}, u32[]{:S(2)}, u32[]{:S(2)}) async-start(bf16[4,192,864]{2,1,0:T(8,128)(2,1)} %pad_maximum_fusion.10), calls=%async_computation.5 | async-start | bytes 2752512 | tf_op jit(solution)/shard_map/all_to_all | solution.py:361
  757.6 65.9 %collective-permute-start.68 = (bf16[128,2304]{1,0:T(8,128)(2,1)}, bf16[128,2304]{1,0:T(8,128)(2,1)}, u32[]{:S(2)}, u32[]{:S(2)}) collective-permute-start(bf16[128,2304]{1,0:T(8,128)(2,1)} %slice.3152), channel_id=1, source_target_pairs={{0,1},{1,0},{2,3},{3,2},{4,5},{5,4},{6,7},{7,6},{8,9},{9,8},{10,11... | collective-permute-start | bytes 1769480 | tf_op jit(solution)/shard_map/ppermute | solution.py:97
  806.4 101.4 %all-to-all-start.6 = ((bf16[4,192,864]{2,1,0:T(8,128)(2,1)}), bf16[4,192,864]{2,1,0:T(8,128)(2,1)}, u32[]{:S(2)}, u32[]{:S(2)}) async-start(bf16[4,192,864]{2,1,0:T(8,128)(2,1)} %pad_maximum_fusion.11), calls=%async_computation.6 | async-start | bytes 2752512 | tf_op jit(solution)/shard_map/all_to_all | solution.py:361
  813.0 68.3 %collective-permute-start.96 = (bf16[576,1152]{1,0:T(8,128)(2,1)}, bf16[576,1152]{1,0:T(8,128)(2,1)S(1)}, u32[]{:S(2)}, u32[]{:S(2)}) collective-permute-start(bf16[576,1152]{1,0:T(8,128)(2,1)} %pad_maximum_fusion.18), channel_id=1, source_target_pairs={{0,16},{8,24},{16,0},{24,8},{1,17},{9,25},{17,1},{25,9},{2,18},{10... | collective-permute-start | bytes 3981320 | tf_op jit(solution)/shard_map/ppermute | solution.py:148
  819.1 64.6 %collective-permute-start.94 = (bf16[576,1152]{1,0:T(8,128)(2,1)S(1)}, bf16[576,1152]{1,0:T(8,128)(2,1)S(1)}, u32[]{:S(2)}, u32[]{:S(2)}) collective-permute-start(bf16[576,1152]{1,0:T(8,128)(2,1)S(1)} %copy-done.67), channel_id=1, source_target_pairs={{0,8},{8,0},{16,24},{24,16},{1,9},{9,1},{17,25},{25,17},{2,10},{10... | collective-permute-start | bytes 3981320 | tf_op jit(solution)/shard_map/ppermute | solution.py:148
  820.5 44.8 %collective-permute-start.85 = (bf16[576,768]{1,0:T(8,128)(2,1)S(1)}, bf16[576,768]{1,0:T(8,128)(2,1)S(1)}, u32[]{:S(2)}, u32[]{:S(2)}) collective-permute-start(bf16[576,768]{1,0:T(8,128)(2,1)S(1)} %pad_maximum_fusion.34), channel_id=1, source_target_pairs={{0,16},{8,24},{16,0},{24,8},{1,17},{9,25},{17,1},{25,9},{2,18},{10... | collective-permute-start | bytes 2654216 | tf_op jit(solution)/shard_map/ppermute | solution.py:148
  823.5 44.4 %collective-permute-start.83 = (bf16[576,768]{1,0:T(8,128)(2,1)S(1)}, bf16[576,768]{1,0:T(8,128)(2,1)S(1)}, u32[]{:S(2)}, u32[]{:S(2)}) collective-permute-start(bf16[576,768]{1,0:T(8,128)(2,1)S(1)} %pad_maximum_fusion.33), channel_id=1, source_target_pairs={{0,8},{8,0},{16,24},{24,16},{1,9},{9,1},{17,25},{25,17},{2,10},{10... | collective-permute-start | bytes 2654216 | tf_op jit(solution)/shard_map/ppermute | solution.py:148
  849.8 53.7 %collective-permute-start.92 = (bf16[576,1024]{1,0:T(8,128)(2,1)S(1)}, bf16[576,1024]{1,0:T(8,128)(2,1)S(1)}, u32[]{:S(2)}, u32[]{:S(2)}) collective-permute-start(bf16[576,1024]{1,0:T(8,128)(2,1)S(1)} %pad_maximum_fusion.29), channel_id=1, source_target_pairs={{0,16},{8,24},{16,0},{24,8},{1,17},{9,25},{17,1},{25,9},{2,18},{10... | collective-permute-start | bytes 3538952 | tf_op jit(solution)/shard_map/ppermute | solution.py:148
  865.3 38.3 %collective-permute-start.90 = (bf16[576,1024]{1,0:T(8,128)(2,1)S(1)}, bf16[576,1024]{1,0:T(8,128)(2,1)S(1)}, u32[]{:S(2)}, u32[]{:S(2)}) collective-permute-start(bf16[576,1024]{1,0:T(8,128)(2,1)S(1)} %pad_maximum_fusion.28), channel_id=1, source_target_pairs={{0,8},{8,0},{16,24},{24,16},{1,9},{9,1},{17,25},{25,17},{2,10},{10... | collective-permute-start | bytes 3538952 | tf_op jit(solution)/shard_map/ppermute | solution.py:148
  891.7 55.9 %collective-permute-start.80 = (bf16[128,2304]{1,0:T(8,128)(2,1)}, bf16[128,2304]{1,0:T(8,128)(2,1)}, u32[]{:S(2)}, u32[]{:S(2)}) collective-permute-start(bf16[128,2304]{1,0:T(8,128)(2,1)} %slice.3150), channel_id=1, source_target_pairs={{0,1},{1,0},{2,3},{3,2},{4,5},{5,4},{6,7},{7,6},{8,9},{9,8},{10,11... | collective-permute-start | bytes 1769480 | tf_op jit(solution)/shard_map/ppermute | solution.py:97
  928.1 71.1 %all-to-all-start.7 = ((bf16[4,192,864]{2,1,0:T(8,128)(2,1)}), bf16[4,192,864]{2,1,0:T(8,128)(2,1)}, u32[]{:S(2)}, u32[]{:S(2)}) async-start(bf16[4,192,864]{2,1,0:T(8,128)(2,1)} %pad_maximum_fusion.12), calls=%async_computation.7 | async-start | bytes 2752512 | tf_op jit(solution)/shard_map/all_to_all | solution.py:361
  977.4 176.7 %collective-permute-start.81 = (f32[128,2304]{1,0:T(8,128)}, f32[128,2304]{1,0:T(8,128)}, u32[]{:S(2)}, u32[]{:S(2)}) collective-permute-start(f32[128,2304]{1,0:T(8,128)} %fusion.119), channel_id=1, source_target_pairs={{0,1},{1,0},{2,3},{3,2},{4,5},{5,4},{6,7},{7,6},{8,9},{9,8},{10,11... | collective-permute-start | bytes 3538952 | tf_op jit(solution)/shard_map/ppermute | solution.py:97
  (246 other events, 3316.2 us)

commit v2 on v1

--- a/solution.py
+++ b/solution.py
@@ -545,30 +545,38 @@
         for value in (left_stats, right_stats, left_roots, right_roots)
     )
     in_blocks = attention_input_master.shape[1] // SUBW
-    out_count = attn_out.shape[1] // SUBW
     ffn_blocks = ffn_cols // SUBW
-    first = in_blocks + out_count
-    masters = (attention_input_master, attn_out, mlp_in, mlp_out)
-    grads = (grad_attn_in, out_grad, grad_mlp_in, down_grad)
-    pieces = [
-        jnp.transpose(grad.reshape(dblock, grad.shape[1] // SUBW, SUBW), (1, 0, 2))
-        for grad in grads
-    ]
-    stacked = low(jnp.concatenate(pieces, axis=0))
+    first = in_blocks + attn_out.shape[1] // SUBW
     batched = lambda left, right, sum_left, sum_right: lax.dot_general(
         left, right, (((sum_left,), (sum_right,)), ((0,), (0,))), preferred_element_type=jnp.float32
     )
+
+    def blocks_of(grad):
+        split = grad.reshape(dblock, grad.shape[1] // SUBW, SUBW)
+        return jnp.transpose(low(split), (1, 0, 2))
+
+    def renew(master, blocks, start):
+        span = slice(start, start + blocks.shape[0])
+        step = batched(low(batched(low(stats[2][span]), blocks, 2, 1)), low(stats[3][span]), 2, 1)
+        return master - master_rate * jnp.transpose(step, (1, 0, 2)).reshape(master.shape)
+
+    down_blocks = blocks_of(down_grad)
+    new_mlp_out = renew(mlp_out, down_blocks, first + 2 * ffn_blocks)
+    gate_blocks = blocks_of(gate_grad_whole)
+    up_blocks = blocks_of(up_grad_whole)
+    new_mlp_in = jnp.concatenate(
+        [
+            renew(mlp_in[:, :ffn_cols], gate_blocks, first),
+            renew(mlp_in[:, ffn_cols:], up_blocks, first + ffn_blocks),
+        ],
+        axis=1,
+    )
+    pieces = [blocks_of(grad) for grad in (grad_attn_in, out_grad)]
+    stacked = jnp.concatenate(pieces + [gate_blocks, up_blocks, down_blocks], axis=0)
     new_left = stat_decay * stats[0] + (1.0 - stat_decay) * batched(stacked, stacked, 2, 2)
     new_right = stat_decay * stats[1] + (1.0 - stat_decay) * batched(stacked, stacked, 1, 1)
-    step = batched(low(batched(low(stats[2]), stacked, 2, 1)), low(stats[3]), 2, 1)
-    updated = []
-    offset = 0
-    for master in masters:
-        count = master.shape[1] // SUBW
-        part = jnp.transpose(step[offset : offset + count], (1, 0, 2))
-        updated.append(master - master_rate * part.reshape(dblock, master.shape[1]))
-        offset = offset + count
-    new_attn_in, new_attn_out, new_mlp_in, new_mlp_out = updated
+    new_attn_in = renew(attention_input_master, pieces[0], 0)
+    new_attn_out = renew(attn_out, pieces[1], in_blocks)
     return (
         block_out,
         input_grad,

time: 1170 us -> 1190 us (1.017)
  waiting for transfers between devices: 269 us -> 282 us
    ppermute x40, waiting for transfers between devices: 63.1 us -> 121 us  [neighbour(): return lax.ppermute(block, 'dp', [(i, i ^ bit) for i in range(4)])]
    ppermute x36, waiting for transfers between devices: 150 us -> 115 us  [cycle(): lax.ppermute(block, axis, [(i, (i + distance) % count) for i in range(cou...]
    another operation x13 -> x14, other arithmetic: 32.2 us -> 55.4 us
    unnamed x353 -> x347, local copies, waits for them, and re-layouts: 60.1 us -> 48.5 us
    dot_general x3 -> x7, matrix products: 62.5 us -> 70.3 us  [body(): lax.dot_general(left, right, (((sum_left,), (sum_right,)), ((0,), (0,))),...]
  transfers between devices with their start and end apart: 115 -> 115, of which waited for: 41 -> 46; matrix products, arithmetic and copies ran while one was open for 55% -> 56% of each run, Pallas kernels for 0% -> 0%
where the time goes in v2:
time: 1190 us; the launch traced here: 1180 us
  other arithmetic  285 us (24%)
  waiting for transfers between devices  282 us (24%)
  matrix products  232 us (19%)
  local copies, waits for them, and re-layouts  204 us (17%)
  starting transfers between devices  171 us (14%)
    ppermute x40, waiting for transfers between devices, neighbour(): return lax.ppermute(block, 'dp', [(i, i ^ bit) for i in range(4)])  121 us
    ppermute x36, waiting for transfers between devices, cycle(): lax.ppermute(block, axis, [(i, (i + distance) % count) for i in range(cou...  115 us
    ppermute x36, starting transfers between devices, cycle(): lax.ppermute(block, axis, [(i, (i + distance) % count) for i in range(cou...  77.9 us
    dot_general x7, matrix products, body(): lax.dot_general(left, right, (((sum_left,), (sum_right,)), ((0,), (0,))),...  70.3 us
    dot_general x23, matrix products, dot_nt(): lax.dot_general(left, right, (((1,), (1,)), ((), ())), preferred_element_...  65.8 us
    dot_general x21, matrix products, dot(): lax.dot_general(left, right, (((1,), (0,)), ((), ())), preferred_element_...  59.3 us
    another operation x14, other arithmetic  55.4 us
    unnamed x347, local copies, waits for them, and re-layouts  48.5 us
  transfers between devices with their start and end apart: 115, of which 46 were waited for; matrix products, arithmetic and copies ran while one was open for 56% of the time, Pallas kernels for 0%

profile of v2, /device:TPU:0, one launch (start us, length us, event | category | flops | bytes accessed | tf_op | source)
XLA Modules:
  0.0 1178.7 jit_solution(575359524234089996)
XLA Ops:
  46.1 24.9 %convert.280 = bf16[1,1,1,33,576,576]{5,4,3,2,1,0:T(8,128)(2,1)} convert(f32[1,1,1,33,576,576]{5,4,3,2,1,0:T(8,128)} %param.28) | non-fusion elementwise | flops 10948608 | bytes 65691648 | tf_op jit(solution)/shard_map/convert.15
  104.1 9.2 collective-permute-done.5
  131.6 6.8 fusion.258
  138.6 6.8 fusion.259
  161.7 11.2 collective-permute-done.3
  178.2 7.9 fusion.232
  194.2 16.5 %collective-permute-start.11 = (bf16[128,2304]{1,0:T(8,128)(2,1)S(1)}, bf16[128,2304]{1,0:T(8,128)(2,1)}, u32[]{:S(2)}, u32[]{:S(2)}) collective-permute-start(bf16[128,2304]{1,0:T(8,128)(2,1)S(1)} %collective-permute-done.9), channel_id=1, source_target_pairs={{0,2},{2,4},{4,6},{6,0},{1,3},{3,5},{5,7},{7,1},{8,10},{10,12},{12... | collective-permute-start | bytes 1769480 | tf_op jit(solution)/shard_map/ppermute | solution.py:102
  223.0 18.0 %collective-permute-start.13 = (bf16[128,2304]{1,0:T(8,128)(2,1)}, bf16[128,2304]{1,0:T(8,128)(2,1)}, u32[]{:S(2)}, u32[]{:S(2)}) collective-permute-start(bf16[128,2304]{1,0:T(8,128)(2,1)} %collective-permute-done.11), channel_id=1, source_target_pairs={{0,2},{2,4},{4,6},{6,0},{1,3},{3,5},{5,7},{7,1},{8,10},{10,12},{12... | collective-permute-start | bytes 1769480 | tf_op jit(solution)/shard_map/ppermute | solution.py:102
  300.9 6.6 fusion.266
  307.7 6.6 fusion.267
  367.4 6.8 all-to-all-done.2
  399.3 8.1 collective-permute-done.23
  422.8 6.6 collective-permute-done.39
  476.9 9.6 collective-permute-done.42
  489.9 12.7 %collective-permute-done.46 = bf16[128,2304]{1,0:T(8,128)(2,1)S(1)} collective-permute-done((bf16[128,2304]{1,0:T(8,128)(2,1)S(1)}, bf16[128,2304]{1,0:T(8,128)(2,1)S(1)}, u32[]{:S(2)}, u32[]{:S(2)}) %collective-permute-start.46) | collective-permute-done | bytes 589856 | tf_op jit(solution)/shard_map/ppermute | solution.py:102
  573.8 6.7 convolution_convert_fusion.2
  583.9 8.2 convolution_convert_fusion.1
  597.4 8.2 convolution_convert_fusion
  616.1 9.2 collective-permute-done.61
  643.4 40.5 %collective-permute-done.76 = bf16[576,1152]{1,0:T(8,128)(2,1)} collective-permute-done((bf16[576,1152]{1,0:T(8,128)(2,1)}, bf16[576,1152]{1,0:T(8,128)(2,1)}, u32[]{:S(2)}, u32[]{:S(2)}) %collective-permute-start.76) | collective-permute-done | bytes 1327136 | tf_op jit(solution)/shard_map/ppermute | solution.py:148
  730.7 19.7 %collective-permute-done.65 = bf16[1024,512]{1,0:T(8,128)(2,1)S(1)} collective-permute-done((bf16[1024,512]{1,0:T(8,128)(2,1)S(1)}, bf16[1024,512]{1,0:T(8,128)(2,1)S(1)}, u32[]{:S(2)}, u32[]{:S(2)}) %collective-permute-start.65) | collective-permute-done | bytes 1048608 | tf_op jit(solution)/shard_map/ppermute | solution.py:28
  809.0 6.6 multiply_bitcast_fusion
  820.7 6.7 convolution_convert_fusion.4
  846.8 6.7 collective-permute-done.89
  865.8 36.5 %collective-permute-done.85 = bf16[576,768]{1,0:T(8,128)(2,1)S(1)} collective-permute-done((bf16[576,768]{1,0:T(8,128)(2,1)S(1)}, bf16[576,768]{1,0:T(8,128)(2,1)S(1)}, u32[]{:S(2)}, u32[]{:S(2)}) %collective-permute-start.85) | collective-permute-done | bytes 884768 | tf_op jit(solution)/shard_map/ppermute | solution.py:148
  926.9 10.4 collective-permute-done.87
  951.3 14.1 %collective-permute-done.90 = bf16[576,1024]{1,0:T(8,128)(2,1)} collective-permute-done((bf16[576,1024]{1,0:T(8,128)(2,1)}, bf16[576,1024]{1,0:T(8,128)(2,1)}, u32[]{:S(2)}, u32[]{:S(2)}) %collective-permute-start.90) | collective-permute-done | bytes 1179680 | tf_op jit(solution)/shard_map/ppermute | solution.py:148
  1016.4 12.5 %collective-permute-done.79 = bf16[128,2304]{1,0:T(8,128)(2,1)} collective-permute-done((bf16[128,2304]{1,0:T(8,128)(2,1)}, bf16[128,2304]{1,0:T(8,128)(2,1)}, u32[]{:S(2)}, u32[]{:S(2)}) %collective-permute-start.79) | collective-permute-done | bytes 589856 | tf_op jit(solution)/shard_map/ppermute | solution.py:102
  1056.1 7.2 add_convert_fusion.17
  1095.5 7.0 multiply_bitcast_fusion.1
  1125.9 37.3 %fusion.1 = f32[1,1,1,33,576,576]{5,4,3,2,1,0:T(8,128)} fusion(f32[1,1,1,33,576,576]{5,4,3,2,1,0:T(8,128)} %param.26, bf16[33,576,128]{2,1,0:T(8,128)(2,1)} %bitcast_dynamic-update-slice_fusion), kind=kOutput, calls=%fused_computation.2 | convolution fusion | flops 2824740864 | bytes 92454912 | tf_op jit(solution)/shard_map/dot_general | solution.py:550
  1168.2 7.0 fusion.43
  (972 shorter events, 771.4 us)
Async XLA Ops:
  2.8 72.4 %collective-permute-start = (bf16[576,256]{1,0:T(8,128)(2,1)}, bf16[576,256]{1,0:T(8,128)(2,1)S(1)}, u32[]{:S(2)}, u32[]{:S(2)}) collective-permute-start(bf16[576,256]{1,0:T(8,128)(2,1)} %slice.2529), channel_id=1, source_target_pairs={{0,2},{2,4},{4,6},{6,0},{1,3},{3,5},{5,7},{7,1},{8,10},{10,12},{12... | collective-permute-start | bytes 884744 | tf_op jit(solution)/shard_map/ppermute | solution.py:102
  5.9 69.4 %collective-permute-start.1 = (bf16[576,256]{1,0:T(8,128)(2,1)}, bf16[576,256]{1,0:T(8,128)(2,1)}, u32[]{:S(2)}, u32[]{:S(2)}) collective-permute-start(bf16[576,256]{1,0:T(8,128)(2,1)} %slice.2529), channel_id=1, source_target_pairs={{0,4},{2,6},{4,0},{6,2},{1,5},{3,7},{5,1},{7,3},{8,12},{10,14},{12... | collective-permute-start | bytes 884744 | tf_op jit(solution)/shard_map/ppermute | solution.py:102
  8.5 66.8 %collective-permute-start.2 = (bf16[576,256]{1,0:T(8,128)(2,1)}, bf16[576,256]{1,0:T(8,128)(2,1)}, u32[]{:S(2)}, u32[]{:S(2)}) collective-permute-start(bf16[576,256]{1,0:T(8,128)(2,1)} %slice.2529), channel_id=1, source_target_pairs={{0,6},{2,0},{4,2},{6,4},{1,7},{3,1},{5,3},{7,5},{8,14},{10,8},{12,... | collective-permute-start | bytes 884744 | tf_op jit(solution)/shard_map/ppermute | solution.py:102
  152.9 61.6 %collective-permute-start.25 = (bf16[576,1152]{1,0:T(8,128)(2,1)}, bf16[576,1152]{1,0:T(8,128)(2,1)S(1)}, u32[]{:S(2)}, u32[]{:S(2)}) collective-permute-start(bf16[576,1152]{1,0:T(8,128)(2,1)} %concatenate.451), channel_id=1, source_target_pairs={{0,8},{8,0},{16,24},{24,16},{1,9},{9,1},{17,25},{25,17},{2,10},{10... | collective-permute-start | bytes 3981320 | tf_op jit(solution)/shard_map/ppermute | solution.py:148
  153.5 62.3 %collective-permute-start.26 = (bf16[576,1152]{1,0:T(8,128)(2,1)}, bf16[576,1152]{1,0:T(8,128)(2,1)S(1)}, u32[]{:S(2)}, u32[]{:S(2)}) collective-permute-start(bf16[576,1152]{1,0:T(8,128)(2,1)} %concatenate.451), channel_id=1, source_target_pairs={{0,16},{8,24},{16,0},{24,8},{1,17},{9,25},{17,1},{25,9},{2,18},{10... | collective-permute-start | bytes 3981320 | tf_op jit(solution)/shard_map/ppermute | solution.py:148
  218.9 38.3 %collective-permute-start.20 = (bf16[288,1024]{1,0:T(8,128)(2,1)}, bf16[288,1024]{1,0:T(8,128)(2,1)}, u32[]{:S(2)}, u32[]{:S(2)}) collective-permute-start(bf16[288,1024]{1,0:T(8,128)(2,1)} %slice.2649), channel_id=1, source_target_pairs={{0,16},{8,24},{16,0},{24,8},{1,17},{9,25},{17,1},{25,9},{2,18},{10... | collective-permute-start | bytes 1769480 | tf_op jit(solution)/shard_map/ppermute | solution.py:148
  222.4 53.8 %collective-permute-start.21 = (bf16[288,1024]{1,0:T(8,128)(2,1)}, bf16[288,1024]{1,0:T(8,128)(2,1)}, u32[]{:S(2)}, u32[]{:S(2)}) collective-permute-start(bf16[288,1024]{1,0:T(8,128)(2,1)} %slice.2650), channel_id=1, source_target_pairs={{0,8},{8,0},{16,24},{24,16},{1,9},{9,1},{17,25},{25,17},{2,10},{10... | collective-permute-start | bytes 1769480 | tf_op jit(solution)/shard_map/ppermute | solution.py:148
  250.1 39.0 %all-to-all-start.1 = ((bf16[4,192,864]{2,1,0:T(8,128)(2,1)}), bf16[4,192,864]{2,1,0:T(8,128)(2,1)}, u32[]{:S(2)}, u32[]{:S(2)}) async-start(bf16[4,192,864]{2,1,0:T(8,128)(2,1)} %pad_maximum_fusion.8), calls=%async_computation.1 | async-start | bytes 2752512 | tf_op jit(solution)/shard_map/all_to_all | solution.py:361
  289.1 37.4 %all-to-all-start.3 = ((bf16[4,192,864]{2,1,0:T(8,128)(2,1)}), bf16[4,192,864]{2,1,0:T(8,128)(2,1)S(1)}, u32[]{:S(2)}, u32[]{:S(2)}) async-start(bf16[4,192,864]{2,1,0:T(8,128)(2,1)} %pad_maximum_fusion.9), calls=%async_computation.3 | async-start | bytes 2752512 | tf_op jit(solution)/shard_map/all_to_all | solution.py:361
  319.9 60.4 %collective-permute-start.29 = (bf16[576,1152]{1,0:T(8,128)(2,1)}, bf16[576,1152]{1,0:T(8,128)(2,1)}, u32[]{:S(2)}, u32[]{:S(2)}) collective-permute-start(bf16[576,1152]{1,0:T(8,128)(2,1)} %concatenate.426), channel_id=1, source_target_pairs={{0,8},{8,0},{16,24},{24,16},{1,9},{9,1},{17,25},{25,17},{2,10},{10... | collective-permute-start | bytes 3981320 | tf_op jit(solution)/shard_map/ppermute | solution.py:148
  322.4 59.7 %collective-permute-start.30 = (bf16[576,1152]{1,0:T(8,128)(2,1)}, bf16[576,1152]{1,0:T(8,128)(2,1)}, u32[]{:S(2)}, u32[]{:S(2)}) collective-permute-start(bf16[576,1152]{1,0:T(8,128)(2,1)} %concatenate.426), channel_id=1, source_target_pairs={{0,16},{8,24},{16,0},{24,8},{1,17},{9,25},{17,1},{25,9},{2,18},{10... | collective-permute-start | bytes 3981320 | tf_op jit(solution)/shard_map/ppermute | solution.py:148
  345.0 44.8 %collective-permute-start.33 = (bf16[576,1152]{1,0:T(8,128)(2,1)}, bf16[576,1152]{1,0:T(8,128)(2,1)}, u32[]{:S(2)}, u32[]{:S(2)}) collective-permute-start(bf16[576,1152]{1,0:T(8,128)(2,1)} %concatenate.439), channel_id=1, source_target_pairs={{0,8},{8,0},{16,24},{24,16},{1,9},{9,1},{17,25},{25,17},{2,10},{10... | collective-permute-start | bytes 3981320 | tf_op jit(solution)/shard_map/ppermute | solution.py:148
  345.5 48.0 %collective-permute-start.34 = (bf16[576,1152]{1,0:T(8,128)(2,1)}, bf16[576,1152]{1,0:T(8,128)(2,1)}, u32[]{:S(2)}, u32[]{:S(2)}) collective-permute-start(bf16[576,1152]{1,0:T(8,128)(2,1)} %concatenate.439), channel_id=1, source_target_pairs={{0,16},{8,24},{16,0},{24,8},{1,17},{9,25},{17,1},{25,9},{2,18},{10... | collective-permute-start | bytes 3981320 | tf_op jit(solution)/shard_map/ppermute | solution.py:148
  519.8 96.3 %collective-permute-start.63 = (bf16[128,2304]{1,0:T(8,128)(2,1)}, bf16[128,2304]{1,0:T(8,128)(2,1)S(1)}, u32[]{:S(2)}, u32[]{:S(2)}) collective-permute-start(bf16[128,2304]{1,0:T(8,128)(2,1)} %slice.3220), channel_id=1, source_target_pairs={{0,1},{1,0},{2,3},{3,2},{4,5},{5,4},{6,7},{7,6},{8,9},{9,8},{10,11... | collective-permute-start | bytes 1769480 | tf_op jit(solution)/shard_map/ppermute | solution.py:97
  610.7 157.9 %collective-permute-start.93 = (bf16[288,1152]{1,0:T(8,128)(2,1)}, bf16[288,1152]{1,0:T(8,128)(2,1)}, u32[]{:S(2)}, u32[]{:S(2)}) collective-permute-start(bf16[288,1152]{1,0:T(8,128)(2,1)} %get-tuple-element.149), channel_id=1, source_target_pairs={{0,16},{8,24},{16,0},{24,8},{1,17},{9,25},{17,1},{25,9},{2,18},{10... | collective-permute-start | bytes 1990664 | tf_op jit(solution)/shard_map/ppermute | solution.py:148
  613.6 155.0 %collective-permute-start.95 = (bf16[288,1152]{1,0:T(8,128)(2,1)}, bf16[288,1152]{1,0:T(8,128)(2,1)}, u32[]{:S(2)}, u32[]{:S(2)}) collective-permute-start(bf16[288,1152]{1,0:T(8,128)(2,1)} %get-tuple-element.151), channel_id=1, source_target_pairs={{0,8},{8,0},{16,24},{24,16},{1,9},{9,1},{17,25},{25,17},{2,10},{10... | collective-permute-start | bytes 1990664 | tf_op jit(solution)/shard_map/ppermute | solution.py:148
  614.2 112.5 %collective-permute-start.72 = (bf16[576,1152]{1,0:T(8,128)(2,1)}, bf16[576,1152]{1,0:T(8,128)(2,1)}, u32[]{:S(2)}, u32[]{:S(2)}) collective-permute-start(bf16[576,1152]{1,0:T(8,128)(2,1)} %pad_maximum_fusion.14), channel_id=1, source_target_pairs={{0,16},{8,24},{16,0},{24,8},{1,17},{9,25},{17,1},{25,9},{2,18},{10... | collective-permute-start | bytes 3981320 | tf_op jit(solution)/shard_map/ppermute | solution.py:148
  628.3 55.6 %collective-permute-start.76 = (bf16[576,1152]{1,0:T(8,128)(2,1)}, bf16[576,1152]{1,0:T(8,128)(2,1)}, u32[]{:S(2)}, u32[]{:S(2)}) collective-permute-start(bf16[576,1152]{1,0:T(8,128)(2,1)} %pad_maximum_fusion.16), channel_id=1, source_target_pairs={{0,16},{8,24},{16,0},{24,8},{1,17},{9,25},{17,1},{25,9},{2,18},{10... | collective-permute-start | bytes 3981320 | tf_op jit(solution)/shard_map/ppermute | solution.py:148
  632.7 52.7 %collective-permute-start.74 = (bf16[576,1152]{1,0:T(8,128)(2,1)}, bf16[576,1152]{1,0:T(8,128)(2,1)}, u32[]{:S(2)}, u32[]{:S(2)}) collective-permute-start(bf16[576,1152]{1,0:T(8,128)(2,1)} %pad_maximum_fusion.15), channel_id=1, source_target_pairs={{0,8},{8,0},{16,24},{24,16},{1,9},{9,1},{17,25},{25,17},{2,10},{10... | collective-permute-start | bytes 3981320 | tf_op jit(solution)/shard_map/ppermute | solution.py:148
  639.3 62.5 %all-to-all-start.4 = ((bf16[4,256,256]{2,1,0:T(8,128)(2,1)}), bf16[4,256,256]{2,1,0:T(8,128)(2,1)}, u32[]{:S(2)}, u32[]{:S(2)}) async-start(bf16[4,256,256]{2,1,0:T(8,128)(2,1)} %pad_maximum_fusion.39), calls=%async_computation.4 | async-start | bytes 1048576 | tf_op jit(solution)/shard_map/all_to_all | solution.py:361
  683.9 42.9 %collective-permute-start.70 = (bf16[576,1152]{1,0:T(8,128)(2,1)}, bf16[576,1152]{1,0:T(8,128)(2,1)}, u32[]{:S(2)}, u32[]{:S(2)}) collective-permute-start(bf16[576,1152]{1,0:T(8,128)(2,1)} %pad_maximum_fusion.13), channel_id=1, source_target_pairs={{0,8},{8,0},{16,24},{24,16},{1,9},{9,1},{17,25},{25,17},{2,10},{10... | collective-permute-start | bytes 3981320 | tf_op jit(solution)/shard_map/ppermute | solution.py:148
  701.8 72.6 %all-to-all-start.5 = ((bf16[4,192,864]{2,1,0:T(8,128)(2,1)}), bf16[4,192,864]{2,1,0:T(8,128)(2,1)}, u32[]{:S(2)}, u32[]{:S(2)}) async-start(bf16[4,192,864]{2,1,0:T(8,128)(2,1)} %pad_maximum_fusion.10), calls=%async_computation.5 | async-start | bytes 2752512 | tf_op jit(solution)/shard_map/all_to_all | solution.py:361
  761.4 255.0 %collective-permute-start.80 = (bf16[128,2304]{1,0:T(8,128)(2,1)}, bf16[128,2304]{1,0:T(8,128)(2,1)}, u32[]{:S(2)}, u32[]{:S(2)}) collective-permute-start(bf16[128,2304]{1,0:T(8,128)(2,1)} %slice.3216), channel_id=1, source_target_pairs={{0,1},{1,0},{2,3},{3,2},{4,5},{5,4},{6,7},{7,6},{8,9},{9,8},{10,11... | collective-permute-start | bytes 1769480 | tf_op jit(solution)/shard_map/ppermute | solution.py:97
  768.1 50.2 %collective-permute-start.66 = (bf16[128,2304]{1,0:T(8,128)(2,1)}, bf16[128,2304]{1,0:T(8,128)(2,1)}, u32[]{:S(2)}, u32[]{:S(2)}) collective-permute-start(bf16[128,2304]{1,0:T(8,128)(2,1)} %slice.3219), channel_id=1, source_target_pairs={{0,1},{1,0},{2,3},{3,2},{4,5},{5,4},{6,7},{7,6},{8,9},{9,8},{10,11... | collective-permute-start | bytes 1769480 | tf_op jit(solution)/shard_map/ppermute | solution.py:97
  801.3 169.0 %all-to-all-start.6 = ((bf16[4,192,864]{2,1,0:T(8,128)(2,1)}), bf16[4,192,864]{2,1,0:T(8,128)(2,1)}, u32[]{:S(2)}, u32[]{:S(2)}) async-start(bf16[4,192,864]{2,1,0:T(8,128)(2,1)} %pad_maximum_fusion.11), calls=%async_computation.6 | async-start | bytes 2752512 | tf_op jit(solution)/shard_map/all_to_all | solution.py:361
  853.5 62.3 %collective-permute-start.96 = (bf16[576,1152]{1,0:T(8,128)(2,1)S(1)}, bf16[576,1152]{1,0:T(8,128)(2,1)S(1)}, u32[]{:S(2)}, u32[]{:S(2)}) collective-permute-start(bf16[576,1152]{1,0:T(8,128)(2,1)S(1)} %copy-done.71), channel_id=1, source_target_pairs={{0,16},{8,24},{16,0},{24,8},{1,17},{9,25},{17,1},{25,9},{2,18},{10... | collective-permute-start | bytes 3981320 | tf_op jit(solution)/shard_map/ppermute | solution.py:148
  854.6 63.7 %collective-permute-start.94 = (bf16[576,1152]{1,0:T(8,128)(2,1)S(1)}, bf16[576,1152]{1,0:T(8,128)(2,1)S(1)}, u32[]{:S(2)}, u32[]{:S(2)}) collective-permute-start(bf16[576,1152]{1,0:T(8,128)(2,1)S(1)} %copy-done.70), channel_id=1, source_target_pairs={{0,8},{8,0},{16,24},{24,16},{1,9},{9,1},{17,25},{25,17},{2,10},{10... | collective-permute-start | bytes 3981320 | tf_op jit(solution)/shard_map/ppermute | solution.py:148
  858.1 44.3 %collective-permute-start.85 = (bf16[576,768]{1,0:T(8,128)(2,1)S(1)}, bf16[576,768]{1,0:T(8,128)(2,1)S(1)}, u32[]{:S(2)}, u32[]{:S(2)}) collective-permute-start(bf16[576,768]{1,0:T(8,128)(2,1)S(1)} %pad_maximum_fusion.34), channel_id=1, source_target_pairs={{0,16},{8,24},{16,0},{24,8},{1,17},{9,25},{17,1},{25,9},{2,18},{10... | collective-permute-start | bytes 2654216 | tf_op jit(solution)/shard_map/ppermute | solution.py:148
  861.1 42.2 %collective-permute-start.83 = (bf16[576,768]{1,0:T(8,128)(2,1)S(1)}, bf16[576,768]{1,0:T(8,128)(2,1)S(1)}, u32[]{:S(2)}, u32[]{:S(2)}) collective-permute-start(bf16[576,768]{1,0:T(8,128)(2,1)S(1)} %pad_maximum_fusion.33), channel_id=1, source_target_pairs={{0,8},{8,0},{16,24},{24,16},{1,9},{9,1},{17,25},{25,17},{2,10},{10... | collective-permute-start | bytes 2654216 | tf_op jit(solution)/shard_map/ppermute | solution.py:148
  902.3 97.8 %collective-permute-start.78 = (bf16[128,2304]{1,0:T(8,128)(2,1)}, bf16[128,2304]{1,0:T(8,128)(2,1)}, u32[]{:S(2)}, u32[]{:S(2)}) collective-permute-start(bf16[128,2304]{1,0:T(8,128)(2,1)} %slice.3217), channel_id=1, source_target_pairs={{0,1},{1,0},{2,3},{3,2},{4,5},{5,4},{6,7},{7,6},{8,9},{9,8},{10,11... | collective-permute-start | bytes 1769480 | tf_op jit(solution)/shard_map/ppermute | solution.py:97
  987.7 68.4 %all-to-all-start.7 = ((bf16[4,192,864]{2,1,0:T(8,128)(2,1)}), bf16[4,192,864]{2,1,0:T(8,128)(2,1)}, u32[]{:S(2)}, u32[]{:S(2)}) async-start(bf16[4,192,864]{2,1,0:T(8,128)(2,1)} %pad_maximum_fusion.12), calls=%async_computation.7 | async-start | bytes 2752512 | tf_op jit(solution)/shard_map/all_to_all | solution.py:361
  1034.2 140.9 %collective-permute-start.81 = (f32[128,2304]{1,0:T(8,128)}, f32[128,2304]{1,0:T(8,128)}, u32[]{:S(2)}, u32[]{:S(2)}) collective-permute-start(f32[128,2304]{1,0:T(8,128)} %fusion.126), channel_id=1, source_target_pairs={{0,1},{1,0},{2,3},{3,2},{4,5},{5,4},{6,7},{7,6},{8,9},{9,8},{10,11... | collective-permute-start | bytes 3538952 | tf_op jit(solution)/shard_map/ppermute | solution.py:97
  (242 other events, 3164.6 us)
